TPU v7x, 256 devices: a whole 4x4x8 slice. The times are simulated.
256 devices in a mesh: sta: 128 (over y, z, x_lo, core), win: 2 (over x_hi).
Axes of the slice: x: 4 (x_hi: 2, x_lo: 2; x = x_hi * 2 + x_lo), y: 4, z: 8, core: 2. Of those that a mesh axis runs over, the one named last changes fastest.
Arguments:
- traces: float32 [256, 4800], P('sta', 'win'), may hold values from -6 to 6
- response_re: float32 [128, 1024], P('sta'), may hold values from -6 to 6
- response_im: float32 [128, 1024], P('sta'), may hold values from -6 to 6
- station_net: int32 [256], P('sta'), may hold values from 0 to 127
- quality: int32 [256, 4], P('sta', 'win'), may hold values 0 or 1
Outputs:
- correlations: float32 [256, 256, 801], P('sta', 'win')
All inputs are finite; a program needn't handle non-finite values. No bound on the sum of `quality` on one device may be relied on, other than what follows from the above.
Results may differ from a plain program's by a relative error of at most 0.0038.
Values may be sent and summed in bfloat16 or wider, within the bound.
A program may use at most 64 MiB of HBM per device.

v0:
```python
import math

import jax
import jax.numpy as jnp
from jax import lax
from jax.sharding import PartitionSpec as P

MAXLAG = 400


def forward_table(seg_len, bins):
    times = jnp.arange(seg_len, dtype=jnp.int32)
    freqs = jnp.arange(bins, dtype=jnp.int32)
    phase = times[:, None] * freqs[None, :] % (2 * bins)
    angle = phase.astype(jnp.float32) * (2.0 * math.pi / (2 * bins))
    return jnp.concatenate([jnp.cos(angle), -jnp.sin(angle)], axis=1)


def inverse_table(bins, maxlag):
    freqs = jnp.arange(bins, dtype=jnp.int32)
    shifts = jnp.arange(2 * maxlag + 1, dtype=jnp.int32) - maxlag + 2 * bins
    phase = freqs[:, None] * shifts[None, :] % (2 * bins)
    angle = phase.astype(jnp.float32) * (2.0 * math.pi / (2 * bins))
    weights = jnp.where(freqs == 0, 1.0, 2.0).astype(jnp.float32) / jnp.sqrt(jnp.float32(bins))
    return jnp.concatenate(
        [weights[:, None] * jnp.cos(angle), -weights[:, None] * jnp.sin(angle)], axis=0
    )


def whiten(rows, resp_re, resp_im, flags, bins):
    spec = jnp.dot(
        rows,
        forward_table(rows.shape[1], bins),
        precision=lax.Precision.HIGHEST,
        preferred_element_type=jnp.float32,
    )
    spec_re, spec_im = (spec[:, :bins], spec[:, bins:])
    power = resp_re * resp_re + resp_im * resp_im
    level = 0.1 * jnp.mean(power, axis=1, keepdims=True) + 1e-06
    denom = power + level
    dec_re = (spec_re * resp_re + spec_im * resp_im) / denom
    dec_im = (spec_im * resp_re - spec_re * resp_im) / denom
    energy = dec_re * dec_re + dec_im * dec_im
    mean_energy = jnp.mean(energy, axis=1, keepdims=True) + 1e-06
    factor = flags[:, None] / jnp.sqrt(energy + 0.5 * mean_energy)
    return jnp.concatenate([dec_re * factor, dec_im * factor], axis=1).astype(jnp.bfloat16)


def cross_spectra(own, other, bins):
    own_re, own_im = (own[:, :, :bins], own[:, :, bins:])
    other_re, other_im = (other[:, :, :bins], other[:, :, bins:])
    cross_re = jnp.einsum(
        "isf,jsf->ijf", own_re, other_re, preferred_element_type=jnp.float32
    ) + jnp.einsum("isf,jsf->ijf", own_im, other_im, preferred_element_type=jnp.float32)
    cross_im = jnp.einsum(
        "isf,jsf->ijf", own_im, other_re, preferred_element_type=jnp.float32
    ) - jnp.einsum("isf,jsf->ijf", own_re, other_im, preferred_element_type=jnp.float32)
    return jnp.concatenate([cross_re, cross_im], axis=2)


def to_lags(cross, table):
    first, second, width = cross.shape
    flat = jnp.dot(
        cross.reshape(first * second, width),
        table,
        precision=lax.Precision.HIGHEST,
        preferred_element_type=jnp.float32,
    )
    return flat.reshape(first, second, table.shape[1])


def on_device(traces, response_re, response_im, station_net, quality):
    sta_dev = traces.shape[0]
    seg_dev = quality.shape[1]
    bins = response_re.shape[1]
    seg_len = traces.shape[1] // seg_dev
    sta_count = lax.axis_size("sta")
    win_count = lax.axis_size("win")
    stations = sta_dev * sta_count
    resp_all_re, resp_all_im = (
        lax.all_gather(response_re, "sta", axis=0, tiled=True),
        lax.all_gather(response_im, "sta", axis=0, tiled=True),
    )
    nets = resp_all_re.shape[0]
    onehot = (station_net[:, None] == jnp.arange(nets, dtype=jnp.int32)[None, :]).astype(
        jnp.float32
    )
    own_re = jnp.dot(
        onehot, resp_all_re, precision=lax.Precision.HIGHEST, preferred_element_type=jnp.float32
    )
    own_im = jnp.dot(
        onehot, resp_all_im, precision=lax.Precision.HIGHEST, preferred_element_type=jnp.float32
    )
    rows = traces.reshape(sta_dev * seg_dev, seg_len)
    flags = quality.reshape(-1).astype(jnp.float32)
    white = whiten(
        rows, jnp.repeat(own_re, seg_dev, axis=0), jnp.repeat(own_im, seg_dev, axis=0), flags, bins
    )
    white = white.reshape(sta_dev, seg_dev, 2 * bins)
    masks_full = lax.all_gather(quality, "win", axis=1, tiled=True)
    own_masks = masks_full.astype(jnp.float32)
    masks_wire = masks_full.astype(jnp.bfloat16)
    table = inverse_table(bins, MAXLAG)
    share = stations // win_count
    spec_piece = lax.all_gather(white, "sta", axis=0, tiled=True)
    mask_piece = lax.all_gather(masks_wire, "sta", axis=0, tiled=True)
    lags = to_lags(cross_spectra(white, spec_piece, bins), table)
    lag_total = lags
    part = jnp.dot(
        own_masks,
        mask_piece.astype(jnp.float32).T,
        precision=lax.Precision.HIGHEST,
        preferred_element_type=jnp.float32,
    )
    lag_total, count_total = (lag_total, part)
    stacked = lax.psum_scatter(lag_total, "win", scatter_dimension=1, tiled=True)
    counts_mine = lax.dynamic_slice_in_dim(count_total, lax.axis_index("win") * share, share, 1)
    return stacked / jnp.maximum(counts_mine, 1.0)[:, :, None]


def solution(mesh):
    return jax.shard_map(
        on_device,
        mesh=mesh,
        in_specs=(P("sta", "win"), P("sta", None), P("sta", None), P("sta"), P("sta", "win")),
        out_specs=P("sta", "win", None),
        check_vma=False,
    )
```

profile of v0, /device:TPU:1, one launch (start us, length us, event | category | flops | bytes accessed | tf_op | source)
XLA Modules:
  0.0 779.7 jit_solution(879382006330741792)
XLA Ops:
  6.5 0.0 all-gather.6.cloned.1.call-start
  6.6 20.7 %sine_negate_fusion = (f32[1200,1024]{1,0:T(8,128)}, f32[1200,1024]{1,0:T(8,128)}) fusion(), kind=kLoop, calls=%fused_computation.17 | loop fusion | flops 18432000 | bytes 9830400 | tf_op jit(solution)/shard_map/neg | solution.py:16
  27.3 0.1 reshape.63
  27.4 162.8 %all-gather = f32[128,1,1024]{2,1,0:T(1,128)S(1)} all-gather(f32[1,1,1024]{2,1,0:T(1,128)S(1)} %bitcast.40), channel_id=1, replica_groups=mesh['sta'=128,'win'=2] {'sta'}, dimensions={0}, use_global_device_ids=true | all-gather | bytes 528384 | tf_op jit(solution)/shard_map/all_gather | solution.py:81
  190.1 0.0 copy-done.8
  190.1 152.5 %all-gather.1 = f32[128,1,1024]{2,1,0:T(1,128)S(1)} all-gather(f32[1,1,1024]{2,1,0:T(1,128)S(1)} %bitcast.41), channel_id=1, replica_groups=mesh['sta'=128,'win'=2] {'sta'}, dimensions={0}, use_global_device_ids=true | all-gather | bytes 528384 | tf_op jit(solution)/shard_map/all_gather | solution.py:82
  342.6 0.3 fusion.29
  342.9 0.4 add_reduce_fusion
  343.4 0.1 reduce_sum.21
  343.5 0.1 add.97
  343.6 0.0 copy-start.9
  343.6 8.3 %fusion.23 = f32[4,2048]{1,0:T(4,128)S(1)} fusion(f32[4,1200]{1,0:T(4,128)S(1)} %reshape.63, f32[1200,1024]{1,0:T(8,128)} %get-tuple-element.20, f32[1200,1024]{1,0:T(8,128)} %get-tuple-element.21), kind=kOutput, calls=%fused_computation.33 | convolution fusion | flops 120422400 | bytes 9882368 | tf_op jit(solution)/shard_map/dot_general | solution.py:31
  352.0 0.2 fusion.33
  352.2 0.1 convert_element_type.32
  352.3 0.1 multiply_convert_fusion.1
  352.4 0.6 pad_maximum_fusion
  353.0 0.0 all-gather.6.cloned.1.call-update
  353.0 0.2 reduce-scatter.2.cloned.1.call-start
  353.3 1.2 copy.18
  354.4 1.2 copy.15
  355.6 15.8 %cosine_multiply_fusion = (f32[1024,801]{0,1:T(8,128)}, f32[1024,801]{0,1:T(8,128)}) fusion(s32[801]{0:T(1024)S(1)} %iota_add_fusion, f32[1024]{0:T(1024)S(1)} %get-tuple-element.18, f32[1024]{0:T(1024)S(1)} %get-tuple-element.19), kind=kLoop, calls=%fused_computation.28 | loop fusion | flops 13123584 | bytes 6573188 | tf_op jit(solution)/shard_map/mul | solution.py:26
  371.4 187.2 %all-gather.6.cloned.1.call-done = bf16[256,2,2048]{2,1,0:T(2,128)(2,1)} async-done(((bf16[2,2,2048]{2,1,0:T(2,128)(2,1)}), bf16[256,2,2048]{2,1,0:T(2,128)(2,1)}) %all-gather.6.cloned.1.call-update) | async-done | bytes 2097168 | tf_op jit(solution)/shard_map/all_gather | solution.py:105
  558.6 2.7 fusion.40
  561.3 2.6 copy.17
  563.9 2.6 copy.14
  566.6 3.9 fusion.43
  570.4 2.6 fusion.45
  573.1 2.6 fusion.42
  575.7 2.7 fusion.44
  578.4 2.8 copy.19
  581.1 4.2 copy.16
  585.3 4.1 copy.21
  589.4 4.1 copy.20
  593.6 2.1 add_bitcast_fusion
  595.7 0.1 copy-done
  595.8 0.6 copy-done.1
  596.4 0.4 subtract_bitcast_fusion
  596.9 0.5 copy-done.3
  597.4 1.2 copy-done.2
  598.6 11.9 %fusion.4 = f32[2,256,801]{1,2,0:T(8,128)} fusion(f32[1024,801]{0,1:T(8,128)S(1)} %copy-done.3, f32[1024,801]{0,1:T(8,128)S(1)} %copy-done.2, f32[2,256,1024]{2,1,0:T(8,128)S(1)} %subtract_bitcast_fusion, f32[2,256,1024]{2,1,0:T(8,128)S(1)} %add_bitcast_fusion), kind=kOutput, calls=%fused_computation.8 | convolution fusion | flops 10081601536 | bytes 12396544 | tf_op jit(solution)/shard_map/dot_general | solution.py:63
  610.5 0.0 reduce-scatter.2.cloned.1.call-update
  610.5 0.1 copy.10
  610.6 4.6 all-gather.2
  615.2 0.1 copy.23
  615.3 154.8 %all-gather.3 = bf16[128,2,4]{2,1,0:T(2,128)(2,1)S(1)} all-gather(bf16[1,2,4]{2,1,0:T(2,128)(2,1)S(1)} %bitcast.45), channel_id=1, replica_groups=mesh['sta'=128,'win'=2] {'sta'}, dimensions={0}, use_global_device_ids=true | all-gather | bytes 2064 | tf_op jit(solution)/shard_map/all_gather | solution.py:106
  770.1 0.2 fusion.46
  770.3 1.3 broadcast_divide_fusion
  771.5 1.3 copy.13
  (30 shorter events, 0.1 us)
Async XLA Ops:
  6.5 20.7 %copy-start.6 = (f32[2,2400]{1,0:T(2,128)S(1)}, f32[2,2400]{1,0:T(2,128)}, u32[]{:S(2)}) copy-start(f32[2,2400]{1,0:T(2,128)} %param.5) | copy-start | bytes 57604
  6.5 20.8 %copy-start.7 = (f32[1,1024]{1,0:T(1,128)S(1)}, f32[1,1024]{1,0:T(1,128)}, u32[]{:S(2)}) copy-start(f32[1,1024]{1,0:T(1,128)} %param.6) | copy-start | bytes 12292
  6.5 183.6 %copy-start.8 = (f32[1,1024]{1,0:T(1,128)S(1)}, f32[1,1024]{1,0:T(1,128)}, u32[]{:S(2)}) copy-start(f32[1,1024]{1,0:T(1,128)} %param.7) | copy-start | bytes 12292
  6.5 336.0 %copy-start.10 = (s32[2]{0:T(128)S(1)}, s32[2]{0:T(128)}, u32[]{:S(2)}) copy-start(s32[2]{0:T(128)} %param.8) | copy-start | bytes 28
  6.5 552.0 %all-gather.6.cloned.1.call-start = ((), (), s32[]{:S(2)}) async-start(), calls=%async_computation.1 | async-start | bytes 2113536 | tf_op jit(solution)/shard_map/all_gather | solution.py:105
  343.6 8.6 %copy-start.9 = (s32[2,2]{1,0:T(2,128)S(1)}, s32[2,2]{1,0:T(2,128)}, u32[]{:S(2)}) copy-start(s32[2,2]{1,0:T(2,128)} %param.9) | copy-start | bytes 52
  353.0 417.2 %reduce-scatter.2.cloned.1.call-start = ((), (), s32[]{:S(2)}) async-start(), calls=%async_computation.2 | async-start | bytes 2482176 | tf_op jit(solution)/shard_map/reduce_scatter | solution.py:116
  566.6 3.9 copy-start.5
  573.1 2.6 copy-start.4
  593.6 2.2 copy-start
  593.6 2.9 copy-start.1
  593.6 3.8 copy-start.3
  596.4 2.2 copy-start.2
Sparse Core Ops, SparseCore 0:
  353.2 205.3 all-gather.5
  610.6 32.8 reduce-scatter.1
where the time goes:
time: 780 us
  blocking collectives  475 us (61%)
  waiting for transfers between devices  187 us (24%)
  other arithmetic  41.2 us (5%)
  matrix products  32.9 us (4%)
  local copies, waits for them, and re-layouts  29.9 us (4%)
  between operations  13.6 us (2%)
    all_gather x1, waiting for transfers between devices, on_device(): spec_piece = lax.all_gather(white, 'sta', axis=0, tiled=True)  187 us
    all_gather x1, blocking collectives, on_device(): lax.all_gather(response_re, 'sta', axis=0, tiled=True)  163 us
    all_gather x1, blocking collectives, on_device(): mask_piece = lax.all_gather(masks_wire, 'sta', axis=0, tiled=True)  155 us
    all_gather x1, blocking collectives, on_device(): lax.all_gather(response_im, 'sta', axis=0, tiled=True)  152 us
    neg x1, other arithmetic, forward_table(): return jnp.concatenate([jnp.cos(angle), -jnp.sin(angle)], axis=1)  20.7 us
    mul x1, other arithmetic, inverse_table(): weights[:, None] * jnp.cos(angle)  15.8 us
  transfers between devices with their start and end apart: 2, of which 1 were waited for; matrix products, arithmetic and copies ran while one was open for 2% of the time, Pallas kernels for 0%

commit v1 on v0

v1 whole, which is shorter than its diff:
```python
import math

import jax
import jax.numpy as jnp
import ml_dtypes
import numpy as np
from jax import lax
from jax.experimental import pallas as pl
from jax.experimental.pallas import tpu as pltpu
from jax.sharding import PartitionSpec as P

MESH = pl.DeviceIdType.MESH
SEG, BINS, MAXLAG = 1200, 1024, 400
FFT = 2 * BINS
LAGS = 2 * MAXLAG + 1
BLOCKS = 7
CHUNKS = ((0, 2), (2, 2), (4, 2), (6, 1))
HIGHEST = lax.Precision.HIGHEST


def tables():
    f1 = np.arange(16)
    lane = np.arange(64)
    f2 = 8 * (lane % 8) + lane // 8
    r = np.arange(128)
    ang = 2 * np.pi * (f1[:, None] * r[None, :] % FFT) / FFT
    twiddle = np.stack([np.cos(ang), -np.sin(ang)]).astype(np.float32)
    ang = 2 * np.pi * (r[:, None] * f2[None, :] % 128) / 128
    c, s = np.cos(ang), np.sin(ang)
    outer = np.concatenate(
        [np.concatenate([c, -s], 1), np.concatenate([s, c], 1)], 0
    ).astype(np.float32)
    f = f1[:, None] + 16 * f2[None, :]
    k = np.arange(LAGS) - MAXLAG
    ang = 2 * np.pi * (f[:, :, None] * k % FFT) / FFT
    w = np.where(f == 0, 1.0, 2.0)[:, :, None] / math.sqrt(BINS)
    inverse = np.zeros((16, 128, BLOCKS * 128), np.float64)
    inverse[:, :64, :LAGS] = w * np.cos(ang)
    inverse[:, 64:, :LAGS] = -w * np.sin(ang)
    return twiddle, outer, inverse.reshape(FFT, BLOCKS * 128).astype(ml_dtypes.bfloat16)


def coords():
    s = lax.axis_index("sta")
    return s // 32, s // 4 % 8, s // 2 % 2, s % 2, lax.axis_index("win")


def device(y, z, xl, c, xh):
    return {"sta": ((y * 8 + z) * 2 + xl) * 2 + c, "win": xh}


def kernel(
    net_ref, qual_ref, tr_ref, re_ref, im_ref, tw_ref, outer_ref, inv_hbm, out_ref,
    inv, xs, lhs, xscr, sq, gbuf, nbuf, csend, crecv, abuf, bbuf, bf, qa, scale, cross, mat, sbuf,
    tsem, s_r1, r_r1, s_n, r_n, s_d, r_d, s_r2, r_r2, s_a, r_a, s_b, r_b, s_o, r_o,
):
    y, z, xl, c, xh = coords()
    me = y * 2 + xl
    lane = lax.broadcasted_iota(jnp.int32, (16, 128), 1)
    low = lane < 64

    def swap(v):
        return pltpu.roll(v, 64, 1)

    def plane(p):
        return device(p // 2, z, p % 2, c, xh)

    def across(p):
        return device(p // 2, z, p % 2, c, 1 - xh)

    half = y // 2
    y_to = y + c * (3 - 2 * y)
    core_to = (1 + xh + half) % 2
    c_from = (y // 2 + xh) % 2
    y_from = y + c_from * (3 - 2 * y)
    xh_from = (1 + c + xh) % 2

    def slot_of(p):
        cb = (p // 4 + xh) % 2
        yb = p // 2 + cb * (3 - 2 * (p // 2))
        return (yb % 2) * 4 + p % 2 * 2 + cb

    barrier = pltpu.get_barrier_semaphore()

    def greet(to):
        pl.semaphore_signal(barrier, inc=1, device_id=to, device_id_type=MESH)

    for d in range(1, 8):
        greet(device(y, (z + d) % 8, xl, c, xh))
        greet(plane((me + d) % 8))
    for d in range(8):
        greet(across((me + d) % 8))
        greet(device(y_from, (z + d) % 8, xl, c_from, xh_from))
    greet(device(y, z, xl, 1 - c, xh))

    table = pltpu.make_async_copy(inv_hbm, inv, tsem)
    table.start()

    sq[...] = jnp.zeros((128, 128), jnp.float32)
    for j in range(8):
        sq[j : j + 1, :] = re_ref[:, 128 * j : 128 * j + 128]
        sq[64 + j : 65 + j, :] = im_ref[:, 128 * j : 128 * j + 128]
    turned = sq[...].T
    resp = turned[0:16, :]
    for m in range(1, 8):
        resp = resp + pltpu.roll(turned[16 * m : 16 * m + 16, :], 8 * m, 1)
    square = resp * resp
    power = square + swap(square)
    level = 0.1 * (jnp.sum(square) / BINS) + 1e-06
    gbuf[c, z] = jnp.where(low, resp, -resp) / (power + level)

    row = lax.broadcasted_iota(jnp.int32, (8, 128), 0)
    nbuf[me] = jnp.where(row < 4, net_ref[0], net_ref[1])

    for q in range(10):
        n = min(128, SEG - 128 * q)
        xs[q] = jnp.zeros((8, 128), jnp.float32)
        xs[q, 0:2, 0:n] = tr_ref[:, 128 * q : 128 * q + n]
        xs[q, 2:4, 0:n] = tr_ref[:, SEG + 128 * q : SEG + 128 * q + n]
    for f in range(9):
        parts = []
        for fn, sign in ((math.cos, 1.0), (math.sin, -1.0)):
            total = jnp.zeros((8, 128), jnp.float32)
            for q in range(10):
                w = sign * fn(2 * math.pi * (f * q % 16) / 16)
                if abs(w) > 1e-9:
                    total = total + (xs[q] if w == 1.0 else xs[q] * w)
            parts.append(total)
        for g in {f, (16 - f) % 16}:
            ar, ai = parts if g == f else (parts[0], -parts[1])
            tr, ti = tw_ref[0, g : g + 1, :], tw_ref[1, g : g + 1, :]
            lhs[8 * g : 8 * g + 8, 0:128] = ar * tr - ai * ti
            lhs[8 * g : 8 * g + 8, 128:256] = ar * ti + ai * tr
    xscr[...] = jnp.dot(
        lhs[...], outer_ref[...], precision=HIGHEST, preferred_element_type=jnp.float32
    )

    pl.semaphore_wait(barrier, 31)

    def remote(src, dst, ssem, rsem, to):
        return pltpu.make_async_remote_copy(
            src_ref=src, dst_ref=dst, send_sem=ssem, recv_sem=rsem, device_id=to,
            device_id_type=MESH,
        )

    sent = []

    def start(copy):
        copy.start()
        sent.append(copy)

    sibling = device(y, z, xl, 1 - c, xh)
    for d in range(1, 8):
        zz = (z + d) % 8
        start(
            remote(gbuf.at[c, z], gbuf.at[c, z], s_r1.at[zz], r_r1.at[z],
                   device(y, zz, xl, c, xh))
        )
    for d in range(1, 8):
        p = (me + d) % 8
        start(remote(nbuf.at[me], nbuf.at[me], s_n.at[p], r_n.at[me], plane(p)))
    for d in range(1, 8):
        zz = (z + d) % 8
        remote(gbuf.at[c, zz], gbuf.at[c, zz], s_r1.at[zz], r_r1.at[zz], sibling).wait_recv()
    start(remote(gbuf.at[c], gbuf.at[c], s_d.at[0], r_d.at[0], sibling))
    for d in range(1, 8):
        p = (me + d) % 8
        remote(nbuf.at[p], nbuf.at[p], s_n.at[p], r_n.at[p], plane(p)).wait_recv()
    remote(gbuf.at[1 - c], gbuf.at[1 - c], s_d.at[0], r_d.at[0], sibling).wait_recv()

    base = y * 32 + xl * 2

    def choose(p):
        want = [nbuf[p, 4 * st : 4 * st + 1, :] for st in range(2)]
        acc = [jnp.zeros((16, 128), jnp.float32) for _ in range(2)]
        for cc in range(2):
            for zz in range(8):
                v = gbuf[cc, zz]
                for st in range(2):
                    acc[st] = jnp.where(want[st] == base + 4 * zz + cc, v, acc[st])
        return acc

    for d in range(1, 8):
        p = (me + d) % 8
        acc = choose(p)
        csend[p, 0], csend[p, 1] = acc[0], acc[1]
        start(remote(csend.at[p], crecv.at[me], s_r2.at[p], r_r2.at[me], plane(p)))
    factors = choose(me)
    for d in range(1, 8):
        p = (me + d) % 8
        remote(csend.at[p], crecv.at[p], s_r2.at[p], r_r2.at[p], plane(p)).wait_recv()
        for st in range(2):
            factors[st] = factors[st] + crecv[p, st]

    own = y * 4 + xh * 2 + xl
    row = lax.broadcasted_iota(jnp.int32, (16, 128), 0)
    marks = jnp.zeros((16, 128), jnp.float32)
    for st in range(2):
        fac = factors[st]
        turn = swap(fac)
        f_re = jnp.where(low, fac, turn)
        f_im = jnp.where(low, -turn, fac)
        for g in range(2):
            spec = xscr[pl.ds(2 * g + st, 16, stride=8), :]
            dec = spec * f_re + swap(spec) * f_im
            square = dec * dec
            energy = square + swap(square)
            mean = jnp.sum(square) / BINS + 1e-06
            flag = qual_ref[st, g].astype(jnp.float32)
            white = dec * (flag / jnp.sqrt(energy + 0.5 * mean))
            abuf[own, 2 * st + g] = white.astype(jnp.bfloat16)
            marks = jnp.where(row // 4 == 2 * st + g, flag, marks)
    abuf[own, 4] = marks.astype(jnp.bfloat16)

    for d in range(8):
        zz = (z + d) % 8
        start(
            remote(abuf.at[own], bbuf.at[xh, z], s_b.at[zz], r_b.at[z],
                   device(y_to, zz, xl, core_to, half))
        )
    for d in range(8):
        p = (me + d) % 8
        if d > 0:
            start(
                remote(abuf.at[own], abuf.at[own], s_a.at[p // 2 * 4 + xh * 2 + p % 2], r_a.at[own],
                       plane(p))
            )
        start(
            remote(abuf.at[own], abuf.at[own], s_a.at[p // 2 * 4 + (1 - xh) * 2 + p % 2],
                   r_a.at[own], across(p))
        )
    for zz in range(8):
        remote(abuf.at[own], bbuf.at[xh_from, zz], s_b.at[zz], r_b.at[zz], sibling).wait_recv()
    start(remote(bbuf.at[xh_from], bbuf.at[xh_from], s_d.at[1], r_d.at[1], sibling))
    for d in range(1, 16):
        s = (own + d) % 16
        remote(abuf.at[own], abuf.at[s], s_a.at[s], r_a.at[s], sibling).wait_recv()
    for p in range(8):
        for x in range(2):
            mark = abuf[p // 2 * 4 + x * 2 + p % 2, 4].astype(jnp.float32)
            for st in range(2):
                for g in range(2):
                    i = 4 * (2 * st + g)
                    qa[2 * x + g, 2 * p + st : 2 * p + st + 1, :] = mark[i : i + 1, :]
    remote(bbuf.at[1 - xh_from], bbuf.at[1 - xh_from], s_d.at[1], r_d.at[1], sibling).wait_recv()

    def second(zz, _):
        marks = [bbuf[x, zz, 4].astype(jnp.float32) for x in range(2)]
        for st in range(2):
            count = jnp.zeros((16, 128), jnp.float32)
            for x in range(2):
                for g in range(2):
                    v = bbuf[x, zz, 2 * st + g].astype(jnp.float32)
                    bf[st * 8 + zz, 2 * x + g, 0] = v
                    bf[st * 8 + zz, 2 * x + g, 1] = swap(v)
                    i = 4 * (2 * st + g)
                    count = count + qa[2 * x + g] * marks[x][i : i + 1, :]
            scale[st * 8 + zz] = 1.0 / jnp.maximum(count, 1.0)
        return 0

    lax.fori_loop(0, 8, second, 0)

    def first(p, _):
        forms = []
        for st in range(2):
            for x in range(2):
                for g in range(2):
                    v = abuf[p // 2 * 4 + x * 2 + p % 2, 2 * st + g].astype(jnp.float32)
                    t = swap(v)
                    forms.append((jnp.where(low, v, -t), jnp.where(low, t, v)))

        def pair(b, _):
            acc = [None, None]
            for s in range(4):
                v, t = bf[b, s, 0], bf[b, s, 1]
                for st in range(2):
                    u, w = forms[4 * st + s]
                    term = u * v + w * t
                    acc[st] = term if acc[st] is None else acc[st] + term
            for st in range(2):
                a = 2 * p + st
                at = pl.multiple_of((a * 16 + b) * 16, 16)
                cross[pl.ds(at, 16), :] = acc[st] * scale[b, pl.ds(a, 1), :]
            return 0

        lax.fori_loop(0, 16, pair, 0, unroll=2)
        return 0

    lax.fori_loop(0, 8, first, 0)
    for f in range(16):
        mat[:, 128 * f : 128 * f + 128] = cross[pl.ds(f, 256, stride=16), :].astype(jnp.bfloat16)

    table.wait()
    mine = slot_of(me)
    for i, (n, count) in enumerate(CHUNKS):
        lags = jnp.dot(
            mat[...], inv[:, 128 * n : 128 * (n + count)], preferred_element_type=jnp.float32
        ).astype(jnp.bfloat16)
        for p in range(8):
            for k in range(count):
                sbuf[p, n + k] = lags[32 * p : 32 * p + 32, 128 * k : 128 * k + 128]
        for d in range(1, 8):
            p = (me + d) % 8
            start(
                remote(sbuf.at[p, pl.ds(n, count)], out_ref.at[mine, pl.ds(n, count)],
                       s_o.at[i, p], r_o.at[i, mine], plane(p))
            )
    keep = pltpu.make_async_copy(sbuf.at[me], out_ref.at[mine], tsem)
    keep.start()
    for i, (n, count) in enumerate(CHUNKS):
        for d in range(1, 8):
            p = (me + d) % 8
            s = slot_of(p)
            remote(sbuf.at[p, pl.ds(n, count)], out_ref.at[s, pl.ds(n, count)],
                   s_o.at[i, p], r_o.at[i, s], plane(p)).wait_recv()
    keep.wait()
    for copy in sent:
        copy.wait_send()


def place(lags_ref, out_ref, rows):
    for n in range(BLOCKS):
        width = min(128, LAGS - 128 * n)
        for a in range(2):
            for s in range(8):
                for st in range(2):
                    at = s // 4 * 64 + s // 2 % 2 * 4 + s % 2 * 2 + st
                    v = lags_ref[s, n, 16 * a + 8 * st : 16 * a + 8 * st + 8, :]
                    rows[pl.ds((2 * n + a) * 128 + at, 8, stride=8), :] = v.astype(jnp.float32)
            v = rows[(2 * n + a) * 128 : (2 * n + a + 1) * 128, :]
            out_ref[a, :, 128 * n : 128 * n + width] = v[:, :width]


def on_device(traces, response_re, response_im, station_net, quality):
    twiddle, outer, inverse = tables()
    f32, bf16 = jnp.float32, jnp.bfloat16
    vmem = pl.BlockSpec(memory_space=pltpu.VMEM)
    smem = pl.BlockSpec(memory_space=pltpu.SMEM)
    dma = pltpu.SemaphoreType.DMA
    lags = pl.pallas_call(
        kernel,
        out_shape=jax.ShapeDtypeStruct((8, BLOCKS, 32, 128), bf16),
        in_specs=[smem, smem, vmem, vmem, vmem, vmem, vmem, pl.BlockSpec(memory_space=pl.ANY)],
        out_specs=pl.BlockSpec(memory_space=pl.ANY),
        scratch_shapes=[
            pltpu.VMEM((FFT, BLOCKS * 128), bf16),
            pltpu.VMEM((10, 8, 128), f32),
            pltpu.VMEM((128, 256), f32),
            pltpu.VMEM((128, 128), f32),
            pltpu.VMEM((128, 128), f32),
            pltpu.VMEM((2, 8, 16, 128), f32),
            pltpu.VMEM((8, 8, 128), jnp.int32),
            pltpu.VMEM((8, 2, 16, 128), f32),
            pltpu.VMEM((8, 2, 16, 128), f32),
            pltpu.VMEM((16, 5, 16, 128), bf16),
            pltpu.VMEM((2, 8, 5, 16, 128), bf16),
            pltpu.VMEM((16, 4, 2, 16, 128), f32),
            pltpu.VMEM((4, 16, 128), f32),
            pltpu.VMEM((16, 16, 128), f32),
            pltpu.VMEM((4096, 128), f32),
            pltpu.VMEM((256, FFT), bf16),
            pltpu.VMEM((8, BLOCKS, 32, 128), bf16),
            dma,
            dma((8,)), dma((8,)), dma((8,)), dma((8,)), dma((2,)), dma((2,)), dma((8,)), dma((8,)),
            dma((16,)), dma((16,)), dma((8,)), dma((8,)), dma((4, 8)), dma((4, 8)),
        ],
        compiler_params=pltpu.CompilerParams(
            collective_id=0, has_side_effects=True, vmem_limit_bytes=40 << 20
        ),
    )(
        station_net, quality, traces, response_re, response_im,
        jnp.asarray(twiddle), jnp.asarray(outer), jnp.asarray(inverse),
    )
    return pl.pallas_call(
        place,
        out_shape=jax.ShapeDtypeStruct((2, 128, LAGS), f32),
        in_specs=[vmem],
        out_specs=vmem,
        scratch_shapes=[pltpu.VMEM((2 * BLOCKS * 128, 128), f32)],
        compiler_params=pltpu.CompilerParams(vmem_limit_bytes=16 << 20),
    )(lags)


def solution(mesh):
    return jax.shard_map(
        on_device,
        mesh=mesh,
        in_specs=(P("sta", "win"), P("sta", None), P("sta", None), P("sta"), P("sta", "win")),
        out_specs=P("sta", "win", None),
        check_vma=False,
    )
```

time: 780 us -> 53.7 us (0.07)
  blocking collectives: 475 us -> 0 us
  waiting for transfers between devices: 187 us -> 0 us
  Pallas kernels: 0 us -> 44.4 us
  other arithmetic: 41.2 us -> 0 us
  matrix products: 32.9 us -> 0 us
  local copies, waits for them, and re-layouts: 29.9 us -> 8.35 us
  between operations: 13.6 us -> 0.02 us
    all_gather x4 -> x0, blocking collectives: 475 us -> none  [the longest x1 163 us: on_device(): lax.all_gather(response_re, 'sta', axis=0, tiled=True)]
    all_gather x1 -> x0, waiting for transfers between devices: 187 us -> none  [on_device(): spec_piece = lax.all_gather(white, 'sta', axis=0, tiled=True)]
    pallas_call x0 -> x2, Pallas kernels: none -> 44.4 us  [the longest x1 44.2 us: on_device(): pl.pallas_call(kernel, out_shape=jax.ShapeDtypeStruct((8, BLOCKS, 32, 128...]
    dot_general x9 -> x0, matrix products: 32.9 us -> none  [the longest x1 11.9 us: to_lags(): jnp.dot(cross.reshape(first * second, width), table, precision=lax.Precis...]
    neg x1 -> x0, other arithmetic: 20.7 us -> none  [forward_table(): return jnp.concatenate([jnp.cos(angle), -jnp.sin(angle)], axis=1)]
    mul x2 -> x0, other arithmetic: 15.8 us -> none  [the longest x1 15.8 us: inverse_table(): weights[:, None] * jnp.cos(angle)]
    dot_general x4 -> x0, local copies, waits for them, and re-layouts: 15.2 us -> none  [the longest x1 4.2 us: cross_spectra(): jnp.einsum('isf,jsf->ijf', own_re, other_re, preferred_element_type=jnp.f...]
    slice x3 -> x0, local copies, waits for them, and re-layouts: 7.95 us -> none  [cross_spectra(): other_re, other_im = (other[:, :, :bins], other[:, :, bins:])]
  transfers between devices with their start and end apart: 2 -> 0, of which waited for: 1 -> 0; matrix products, arithmetic and copies ran while one was open for 2% -> 0% of each run, Pallas kernels for 0% -> 0%
where the time goes in v1:
time: 53.7 us; the launch traced here: 52.8 us
  Pallas kernels  44.4 us (83%)
  local copies, waits for them, and re-layouts  8.35 us (16%)
    pallas_call x1, Pallas kernels, on_device(): pl.pallas_call(kernel, out_shape=jax.ShapeDtypeStruct((8, BLOCKS, 32, 128...  44.2 us
    unnamed x16, local copies, waits for them, and re-layouts  7.09 us
    pallas_call x1, local copies, waits for them, and re-layouts, on_device(): pl.pallas_call(place, out_shape=jax.ShapeDtypeStruct((2, 128, LAGS), f32)...  1.26 us

profile of v1, /device:TPU:1, one launch (start us, length us, event | category | flops | bytes accessed | tf_op | source)
XLA Modules:
  0.0 52.8 jit_solution(12694237647955996930)
XLA Ops:
  0.0 0.0 copy-start
  0.0 2.0 %copy-done = bf16[2048,896]{1,0:T(8,128)(2,1)S(1)} copy-done((bf16[2048,896]{1,0:T(8,128)(2,1)S(1)}, bf16[2048,896]{1,0:T(8,128)(2,1)}, u32[]{:S(2)}) %copy-start) | copy-done | bytes 3670040
  2.0 0.0 copy-start.1
  2.0 0.9 %copy-done.1 = f32[256,128]{1,0:T(8,128)S(1)} copy-done((f32[256,128]{1,0:T(8,128)S(1)}, f32[256,128]{1,0:T(8,128)}, u32[]{:S(2)}) %copy-start.1) | copy-done | bytes 131096
  2.9 0.0 copy-start.2
  2.9 0.7 %copy-done.2 = f32[2,2400]{1,0:T(2,128)S(1)} copy-done((f32[2,2400]{1,0:T(2,128)S(1)}, f32[2,2400]{1,0:T(2,128)}, u32[]{:S(2)}) %copy-start.2) | copy-done | bytes 19224
  3.7 0.0 copy-start.3
  3.7 0.7 %copy-done.3 = f32[2,16,128]{2,1,0:T(8,128)S(1)} copy-done((f32[2,16,128]{2,1,0:T(8,128)S(1)}, f32[2,16,128]{2,1,0:T(8,128)}, u32[]{:S(2)}) %copy-start.3) | copy-done | bytes 16408
  4.4 0.0 copy-start.4
  4.4 0.7 %copy-done.4 = f32[1,1024]{1,0:T(1,128)S(1)} copy-done((f32[1,1024]{1,0:T(1,128)S(1)}, f32[1,1024]{1,0:T(1,128)}, u32[]{:S(2)}) %copy-start.4) | copy-done | bytes 4120
  5.1 0.0 copy-start.5
  5.1 0.7 %copy-done.5 = f32[1,1024]{1,0:T(1,128)S(1)} copy-done((f32[1,1024]{1,0:T(1,128)S(1)}, f32[1,1024]{1,0:T(1,128)}, u32[]{:S(2)}) %copy-start.5) | copy-done | bytes 4120
  5.8 0.0 copy-start.6
  5.8 0.7 %copy-done.6 = s32[2,2]{1,0:T(2,128)S(1)} copy-done((s32[2,2]{1,0:T(2,128)S(1)}, s32[2,2]{1,0:T(2,128)}, u32[]{:S(2)}) %copy-start.6) | copy-done | bytes 40
  6.4 0.0 copy-start.7
  6.4 0.7 %copy-done.7 = s32[2]{0:T(128)S(1)} copy-done((s32[2]{0:T(128)S(1)}, s32[2]{0:T(128)}, u32[]{:S(2)}) %copy-start.7) | copy-done | bytes 32
  7.1 44.2 %shard_map.82.lags_ref = bf16[8,7,32,128]{3,2,1,0:T(8,128)(2,1)S(1)} custom-call(s32[2]{0:T(128)S(1)} %copy-done.7, s32[2,2]{1,0:T(2,128)S(1)} %copy-done.6, f32[2,2400]{1,0:T(2,128)S(1)} %copy-done.2, f32[1,1024]{1,0:T(1,128)S(1)} %copy-done.4, f32[1,1024]{1,0:T(1,128)S(1)} %copy-done.5, f32[2,16,128]{2,1,0:T(8,128)S(1)} %copy-done.3, ...), custom_call_target="tpu_custom_call" | custom-call | tf_op jit(solution)/shard_map/pallas_call | solution.py:340
  51.3 0.2 shard_map.83
  51.5 1.3 %copy.9 = f32[2,128,801]{1,0,2:T(2,128)} copy(f32[2,128,801]{2,1,0:T(8,128)S(1)} %shard_map.83) | data formatting | bytes 1640448 | tf_op jit(solution)/shard_map/pallas_call | solution.py:374
Async XLA Ops:
  0.0 2.0 %copy-start = (bf16[2048,896]{1,0:T(8,128)(2,1)S(1)}, bf16[2048,896]{1,0:T(8,128)(2,1)}, u32[]{:S(2)}) copy-start(bf16[2048,896]{1,0:T(8,128)(2,1)} %constant.8.clone.inv_hbm) | copy-start | bytes 11010052
  2.0 0.9 %copy-start.1 = (f32[256,128]{1,0:T(8,128)S(1)}, f32[256,128]{1,0:T(8,128)}, u32[]{:S(2)}) copy-start(f32[256,128]{1,0:T(8,128)} %constant.7.clone.outer_ref) | copy-start | bytes 393220
  2.9 0.7 %copy-start.2 = (f32[2,2400]{1,0:T(2,128)S(1)}, f32[2,2400]{1,0:T(2,128)}, u32[]{:S(2)}) copy-start(f32[2,2400]{1,0:T(2,128)} %tr_ref.1) | copy-start | bytes 57604
  3.7 0.7 %copy-start.3 = (f32[2,16,128]{2,1,0:T(8,128)S(1)}, f32[2,16,128]{2,1,0:T(8,128)}, u32[]{:S(2)}) copy-start(f32[2,16,128]{2,1,0:T(8,128)} %constant.6.clone.tw_ref) | copy-start | bytes 49156
  4.4 0.7 %copy-start.4 = (f32[1,1024]{1,0:T(1,128)S(1)}, f32[1,1024]{1,0:T(1,128)}, u32[]{:S(2)}) copy-start(f32[1,1024]{1,0:T(1,128)} %re_ref.1) | copy-start | bytes 12292
  5.1 0.7 %copy-start.5 = (f32[1,1024]{1,0:T(1,128)S(1)}, f32[1,1024]{1,0:T(1,128)}, u32[]{:S(2)}) copy-start(f32[1,1024]{1,0:T(1,128)} %im_ref.1) | copy-start | bytes 12292
  5.8 0.7 %copy-start.6 = (s32[2,2]{1,0:T(2,128)S(1)}, s32[2,2]{1,0:T(2,128)}, u32[]{:S(2)}) copy-start(s32[2,2]{1,0:T(2,128)} %qual_ref.1) | copy-start | bytes 52
  6.4 0.7 %copy-start.7 = (s32[2]{0:T(128)S(1)}, s32[2]{0:T(128)}, u32[]{:S(2)}) copy-start(s32[2]{0:T(128)} %net_ref.1) | copy-start | bytes 28

commit v2 on v1

--- a/solution.py
+++ b/solution.py
@@ -50,9 +50,9 @@
 
 
 def kernel(
-    net_ref, qual_ref, tr_ref, re_ref, im_ref, tw_ref, outer_ref, inv_hbm, out_ref,
-    inv, xs, lhs, xscr, sq, gbuf, nbuf, csend, crecv, abuf, bbuf, bf, qa, scale, cross, mat, sbuf,
-    tsem, s_r1, r_r1, s_n, r_n, s_d, r_d, s_r2, r_r2, s_a, r_a, s_b, r_b, s_o, r_o,
+    net_hbm, qual_hbm, tr_hbm, re_hbm, im_hbm, tw_hbm, outer_hbm, inv_hbm, out_ref,
+    net_ref, qual_ref, tr_ref, re_ref, im_ref, tw_ref, outer_ref, inv, xs, lhs, xscr, sq, gbuf, nbuf, csend, crecv, abuf, bbuf, bf, qa, scale, cross, mat, sbuf,
+    isem, tsem, s_r1, r_r1, s_n, r_n, s_d, r_d, s_r2, r_r2, s_a, r_a, s_b, r_b, s_o, r_o,
 ):
     y, z, xl, c, xh = coords()
     me = y * 2 + xl
@@ -80,6 +80,18 @@
         yb = p // 2 + cb * (3 - 2 * (p // 2))
         return (yb % 2) * 4 + p % 2 * 2 + cb
 
+    loads = [
+        pltpu.make_async_copy(src, dst, isem.at[i])
+        for i, (src, dst) in enumerate(
+            (
+                (re_hbm, re_ref), (im_hbm, im_ref), (tr_hbm, tr_ref), (net_hbm, net_ref),
+                (qual_hbm, qual_ref), (tw_hbm, tw_ref), (outer_hbm, outer_ref),
+            )
+        )
+    ]
+    for load in loads:
+        load.start()
+
     barrier = pltpu.get_barrier_semaphore()
 
     def greet(to):
@@ -88,14 +100,14 @@
     for d in range(1, 8):
         greet(device(y, (z + d) % 8, xl, c, xh))
         greet(plane((me + d) % 8))
-    for d in range(8):
-        greet(across((me + d) % 8))
-        greet(device(y_from, (z + d) % 8, xl, c_from, xh_from))
     greet(device(y, z, xl, 1 - c, xh))
+    greet(across(me))
 
     table = pltpu.make_async_copy(inv_hbm, inv, tsem)
     table.start()
 
+    for load in loads:
+        load.wait()
     sq[...] = jnp.zeros((128, 128), jnp.float32)
     for j in range(8):
         sq[j : j + 1, :] = re_ref[:, 128 * j : 128 * j + 128]
@@ -135,7 +147,7 @@
         lhs[...], outer_ref[...], precision=HIGHEST, preferred_element_type=jnp.float32
     )
 
-    pl.semaphore_wait(barrier, 31)
+    pl.semaphore_wait(barrier, 16)
 
     def remote(src, dst, ssem, rsem, to):
         return pltpu.make_async_remote_copy(
@@ -335,14 +347,20 @@
     twiddle, outer, inverse = tables()
     f32, bf16 = jnp.float32, jnp.bfloat16
     vmem = pl.BlockSpec(memory_space=pltpu.VMEM)
-    smem = pl.BlockSpec(memory_space=pltpu.SMEM)
     dma = pltpu.SemaphoreType.DMA
     lags = pl.pallas_call(
         kernel,
         out_shape=jax.ShapeDtypeStruct((8, BLOCKS, 32, 128), bf16),
-        in_specs=[smem, smem, vmem, vmem, vmem, vmem, vmem, pl.BlockSpec(memory_space=pl.ANY)],
+        in_specs=[pl.BlockSpec(memory_space=pltpu.HBM)] * 8,
         out_specs=pl.BlockSpec(memory_space=pl.ANY),
         scratch_shapes=[
+            pltpu.SMEM(station_net.shape, jnp.int32),
+            pltpu.SMEM(quality.shape, jnp.int32),
+            pltpu.VMEM(traces.shape, f32),
+            pltpu.VMEM(response_re.shape, f32),
+            pltpu.VMEM(response_im.shape, f32),
+            pltpu.VMEM(twiddle.shape, f32),
+            pltpu.VMEM(outer.shape, f32),
             pltpu.VMEM((FFT, BLOCKS * 128), bf16),
             pltpu.VMEM((10, 8, 128), f32),
             pltpu.VMEM((128, 256), f32),
@@ -360,12 +378,12 @@
             pltpu.VMEM((4096, 128), f32),
             pltpu.VMEM((256, FFT), bf16),
             pltpu.VMEM((8, BLOCKS, 32, 128), bf16),
-            dma,
+            dma((7,)), dma,
             dma((8,)), dma((8,)), dma((8,)), dma((8,)), dma((2,)), dma((2,)), dma((8,)), dma((8,)),
             dma((16,)), dma((16,)), dma((8,)), dma((8,)), dma((4, 8)), dma((4, 8)),
         ],
         compiler_params=pltpu.CompilerParams(
-            collective_id=0, has_side_effects=True, vmem_limit_bytes=40 << 20
+            collective_id=0, has_side_effects=True, vmem_limit_bytes=64 << 20
         ),
     )(
         station_net, quality, traces, response_re, response_im,

time: 53.7 us -> 47.1 us (0.88); the launches traced: 52.8 us -> 47 us
  local copies, waits for them, and re-layouts: 8.35 us -> 2.27 us
    unnamed x16 -> x2, local copies, waits for them, and re-layouts: 7.09 us -> 1.01 us
where the time goes in v2:
time: 47.1 us; the launch traced here: 47 us
  Pallas kernels  44.7 us (95%)
  local copies, waits for them, and re-layouts  2.27 us (5%)
    pallas_call x1, Pallas kernels, on_device(): pl.pallas_call(kernel, out_shape=jax.ShapeDtypeStruct((8, BLOCKS, 32, 128...  44.5 us
    pallas_call x1, local copies, waits for them, and re-layouts, on_device(): pl.pallas_call(place, out_shape=jax.ShapeDtypeStruct((2, 128, LAGS), f32)...  1.26 us
    unnamed x2, local copies, waits for them, and re-layouts  1.01 us

profile of v2, /device:TPU:1, one launch (start us, length us, event | category | flops | bytes accessed | tf_op | source)
XLA Modules:
  0.0 47.0 jit_solution(15927431137624492547)
XLA Ops:
  0.0 44.5 %shard_map.82.lags_ref = bf16[8,7,32,128]{3,2,1,0:T(8,128)(2,1)} custom-call(s32[2]{0:T(128)} %net_hbm.1, s32[2,2]{1,0:T(2,128)} %qual_hbm.1, f32[2,2400]{1,0:T(2,128)} %tr_hbm.1, f32[1,1024]{1,0:T(1,128)} %re_hbm.1, f32[1,1024]{1,0:T(1,128)} %im_hbm.1, f32[2,16,128]{2,1,0:T(8,128)} %constant.6.clone.tw_hbm, f32[256,128]{1,0:T(8,128)} %constant.7.clone.outer_hbm, ...), custom_call_target="tpu_custom_call" | custom-call | tf_op jit(solution)/shard_map/pallas_call | solution.py:351
  44.6 0.0 copy-start
  44.6 1.0 %copy-done = bf16[8,7,32,128]{3,2,1,0:T(8,128)(2,1)S(1)} copy-done((bf16[8,7,32,128]{3,2,1,0:T(8,128)(2,1)S(1)}, bf16[8,7,32,128]{3,2,1,0:T(8,128)(2,1)}, u32[]{:S(2)}) %copy-start) | copy-done | bytes 458776
  45.6 0.2 shard_map.83
  45.8 1.3 %copy.9 = f32[2,128,801]{1,0,2:T(2,128)} copy(f32[2,128,801]{2,1,0:T(8,128)S(1)} %shard_map.83) | data formatting | bytes 1640448 | tf_op jit(solution)/shard_map/pallas_call | solution.py:392
Async XLA Ops:
  44.6 1.0 %copy-start = (bf16[8,7,32,128]{3,2,1,0:T(8,128)(2,1)S(1)}, bf16[8,7,32,128]{3,2,1,0:T(8,128)(2,1)}, u32[]{:S(2)}) copy-start(bf16[8,7,32,128]{3,2,1,0:T(8,128)(2,1)} %shard_map.82.lags_ref) | copy-start | bytes 1376260

commit v3 on v2

v3 whole, which is shorter than its diff:
```python
import math

import jax
import jax.numpy as jnp
import ml_dtypes
import numpy as np
from jax import lax
from jax.experimental import pallas as pl
from jax.experimental.pallas import tpu as pltpu
from jax.sharding import PartitionSpec as P

MESH = pl.DeviceIdType.MESH
SEG, BINS, MAXLAG = 1200, 1024, 400
FFT = 2 * BINS
LAGS = 2 * MAXLAG + 1
BLOCKS = 7
CHUNKS = ((0, 2), (2, 2), (4, 2), (6, 1))
GROUPS = ((0, 4), (4, 3))
HIGHEST = lax.Precision.HIGHEST


def tables():
    f1 = np.arange(16)
    lane = np.arange(64)
    f2 = 8 * (lane % 8) + lane // 8
    r = np.arange(128)
    ang = 2 * np.pi * (f1[:, None] * r[None, :] % FFT) / FFT
    twiddle = np.stack([np.cos(ang), -np.sin(ang)]).astype(np.float32)
    ang = 2 * np.pi * (r[:, None] * f2[None, :] % 128) / 128
    c, s = np.cos(ang), np.sin(ang)
    outer = np.concatenate(
        [np.concatenate([c, -s], 1), np.concatenate([s, c], 1)], 0
    ).astype(np.float32)
    f = f1[:, None] + 16 * f2[None, :]
    k = np.arange(LAGS) - MAXLAG
    ang = 2 * np.pi * (f[:, :, None] * k % FFT) / FFT
    w = np.where(f == 0, 1.0, 2.0)[:, :, None] / math.sqrt(BINS)
    inverse = np.zeros((16, 128, BLOCKS * 128), np.float64)
    inverse[:, :64, :LAGS] = w * np.cos(ang)
    inverse[:, 64:, :LAGS] = -w * np.sin(ang)
    return twiddle, outer, inverse.reshape(FFT, BLOCKS * 128).astype(ml_dtypes.bfloat16)


def coords():
    s = lax.axis_index("sta")
    return s // 32, s // 4 % 8, s // 2 % 2, s % 2, lax.axis_index("win")


def device(y, z, xl, c, xh):
    return {"sta": ((y * 8 + z) * 2 + xl) * 2 + c, "win": xh}


def kernel(
    net_hbm, qual_hbm, tr_hbm, re_hbm, im_hbm, tw_hbm, outer_hbm, inv_hbm, out_ref,
    net_ref, qual_ref, tr_ref, re_ref, im_ref, tw_ref, outer_ref, inv,
    xs, lhs, xscr, sq, xsend, xrecv, gbuf, nbuf, csend, crecv, fa, fb, abuf, bbuf, bf, qa, scale, cross, mat, sbuf,
    isem, tsem, s_x, r_x, s_r1, r_r1, s_n, r_n, s_d, r_d, s_r2, r_r2, s_fa, r_fa, s_fb, r_fb, s_a, r_a, s_b, r_b,
    s_o, r_o,
):
    y, z, xl, c, xh = coords()
    me = y * 2 + xl
    own = y * 4 + xh * 2 + xl
    lane = lax.broadcasted_iota(jnp.int32, (16, 128), 1)
    low = lane < 64

    def swap(v):
        return pltpu.roll(v, 64, 1)

    def plane(p):
        return device(p // 2, z, p % 2, c, xh)

    def across(p):
        return device(p // 2, z, p % 2, c, 1 - xh)

    def moved(yy, st):
        return yy + (1 - 2 * (yy % 2)) * (1 - st) + (3 - 2 * yy) * st

    def which(yy, hh):
        return (yy // 2 + hh) % 2

    st_own = which(y, xh)
    home = moved(y, st_own)

    def slot_of(p):
        st = which(p // 2, xh)
        return (moved(p // 2, st) % 2) * 4 + p % 2 * 2 + st

    loads = [
        pltpu.make_async_copy(src, dst, isem.at[i])
        for i, (src, dst) in enumerate(
            (
                (re_hbm, re_ref), (im_hbm, im_ref), (tr_hbm, tr_ref), (net_hbm, net_ref),
                (qual_hbm, qual_ref), (tw_hbm, tw_ref), (outer_hbm, outer_ref),
            )
        )
    ]
    for load in loads:
        load.start()

    barrier = pltpu.get_barrier_semaphore()

    def greet(to):
        pl.semaphore_signal(barrier, inc=1, device_id=to, device_id_type=MESH)

    for d in range(1, 8):
        greet(device(y, (z + d) % 8, xl, c, xh))
        greet(plane((me + d) % 8))
    greet(device(y, z, xl, 1 - c, xh))
    greet(device(home, z, xl, c, 0))
    greet(device(home, z, xl, c, 1))

    table = pltpu.make_async_copy(inv_hbm, inv, tsem)
    table.start()

    for load in loads:
        load.wait()
    sq[...] = jnp.zeros((128, 128), jnp.float32)
    for j in range(8):
        sq[j : j + 1, :] = re_ref[:, 128 * j : 128 * j + 128]
        sq[64 + j : 65 + j, :] = im_ref[:, 128 * j : 128 * j + 128]
    turned = sq[...].T
    resp = turned[0:16, :]
    for m in range(1, 8):
        resp = resp + pltpu.roll(turned[16 * m : 16 * m + 16, :], 8 * m, 1)
    square = resp * resp
    power = square + swap(square)
    level = 0.1 * (jnp.sum(square) / BINS) + 1e-06
    gbuf[c, z] = jnp.where(low, resp, -resp) / (power + level)

    row = lax.broadcasted_iota(jnp.int32, (8, 128), 0)
    nbuf[me] = jnp.where(row < 4, net_ref[0], net_ref[1])

    for q in range(10):
        n = min(128, SEG - 128 * q)
        xs[q] = jnp.zeros((8, 128), jnp.float32)
        xs[q, 0:2, 0:n] = tr_ref[:, 128 * q : 128 * q + n]
        xs[q, 2:4, 0:n] = tr_ref[:, SEG + 128 * q : SEG + 128 * q + n]
    for f in range(9):
        parts = []
        for fn, sign in ((math.cos, 1.0), (math.sin, -1.0)):
            total = jnp.zeros((8, 128), jnp.float32)
            for q in range(10):
                w = sign * fn(2 * math.pi * (f * q % 16) / 16)
                if abs(w) > 1e-9:
                    total = total + (xs[q] if w == 1.0 else xs[q] * w)
            parts.append(total)
        for g in {f, (16 - f) % 16}:
            ar, ai = parts if g == f else (parts[0], -parts[1])
            tr, ti = tw_ref[0, g : g + 1, :], tw_ref[1, g : g + 1, :]
            lhs[8 * g : 8 * g + 8, 0:128] = ar * tr - ai * ti
            lhs[8 * g : 8 * g + 8, 128:256] = ar * ti + ai * tr
    xscr[...] = jnp.dot(
        lhs[...], outer_ref[...], precision=HIGHEST, preferred_element_type=jnp.float32
    )
    group = lax.broadcasted_iota(jnp.int32, (8, 128), 1) // 32
    for st in range(2):
        flags = jnp.zeros((8, 128), jnp.float32)
        for g in range(2):
            flag = qual_ref[st, g].astype(jnp.float32)
            xsend[st, 16 * g : 16 * g + 16] = xscr[pl.ds(2 * g + st, 16, stride=8), :] * flag
            flags = jnp.where(group == 2 * xh + g, flag, flags)
        xsend[st, 32:40] = flags

    pl.semaphore_wait(barrier, 17)

    def remote(src, dst, ssem, rsem, to):
        return pltpu.make_async_remote_copy(
            src_ref=src, dst_ref=dst, send_sem=ssem, recv_sem=rsem, device_id=to,
            device_id_type=MESH,
        )

    sent = []

    def start(copy):
        copy.start()
        sent.append(copy)

    sibling = device(y, z, xl, 1 - c, xh)
    for d in (4, 3, 5, 2, 6, 1, 7):
        zz = (z + d) % 8
        start(
            remote(gbuf.at[c, z], gbuf.at[c, z], s_r1.at[zz], r_r1.at[z],
                   device(y, zz, xl, c, xh))
        )
    for st in range(2):
        start(
            remote(xsend.at[st], xrecv.at[xh], s_x.at[st], r_x.at[xh],
                   device(moved(y, st), z, xl, c, y // 2))
        )
    for d in range(1, 8):
        p = (me + d) % 8
        start(remote(nbuf.at[me], nbuf.at[me], s_n.at[p], r_n.at[me], plane(p)))
    for x in range(2):
        remote(xsend.at[0], xrecv.at[x], s_x.at[0], r_x.at[x], sibling).wait_recv()
    mark = xrecv[0, 32:33, :] + xrecv[1, 32:33, :]
    fa[own] = mark
    fb[c, z] = mark
    for d in range(1, 8):
        zz = (z + d) % 8
        remote(gbuf.at[c, zz], gbuf.at[c, zz], s_r1.at[zz], r_r1.at[zz], sibling).wait_recv()
    start(remote(gbuf.at[c], gbuf.at[c], s_d.at[0], r_d.at[0], sibling))
    for d in range(1, 8):
        zz = (z + d) % 8
        start(remote(fb.at[c, z], fb.at[c, z], s_fb.at[zz], r_fb.at[z], device(y, zz, xl, c, xh)))
    for d in range(1, 8):
        p = (me + d) % 8
        remote(nbuf.at[p], nbuf.at[p], s_n.at[p], r_n.at[p], plane(p)).wait_recv()
    remote(gbuf.at[1 - c], gbuf.at[1 - c], s_d.at[0], r_d.at[0], sibling).wait_recv()

    base = y * 32 + xl * 2

    def choose(p):
        st = which(p // 2, xh)
        want = nbuf[moved(p // 2, st) * 2 + p % 2, pl.ds(4 * st, 1), :]
        acc = jnp.zeros((16, 128), jnp.float32)
        for cc in range(2):
            for zz in range(8):
                acc = jnp.where(want == base + 4 * zz + cc, gbuf[cc, zz], acc)
        return acc

    for d in (4, 5, 3, 2, 6, 1, 7):
        p = (me + d) % 8
        csend[p] = choose(p)
        start(remote(csend.at[p], crecv.at[me], s_r2.at[p], r_r2.at[me], plane(p)))
    factor = choose(me)
    specs = [xrecv[x, 16 * g : 16 * g + 16, :] for x in range(2) for g in range(2)]
    turned = [swap(spec) for spec in specs]
    for d in range(1, 8):
        p = (me + d) % 8
        remote(csend.at[p], crecv.at[p], s_r2.at[p], r_r2.at[p], plane(p)).wait_recv()
        factor = factor + crecv[p]

    turn = swap(factor)
    f_re = jnp.where(low, factor, turn)
    f_im = jnp.where(low, -turn, factor)
    for s in range(4):
        dec = specs[s] * f_re + turned[s] * f_im
        square = dec * dec
        energy = square + swap(square)
        mean = jnp.sum(square) / BINS + 1e-06
        abuf[own, s] = (dec / jnp.sqrt(energy + 0.5 * mean)).astype(jnp.bfloat16)

    for d in (4, 3, 5, 2, 6, 1, 7):
        zz = (z + d) % 8
        start(
            remote(abuf.at[own], bbuf.at[c, z], s_b.at[zz], r_b.at[z], device(y, zz, xl, c, xh))
        )
    for d in (4, 5, 3, 2, 6, 1, 7, 0):
        p = (me + d) % 8
        if d > 0:
            start(
                remote(abuf.at[own], abuf.at[own], s_a.at[p // 2 * 4 + xh * 2 + p % 2], r_a.at[own],
                       plane(p))
            )
        start(
            remote(abuf.at[own], abuf.at[own], s_a.at[p // 2 * 4 + (1 - xh) * 2 + p % 2],
                   r_a.at[own], across(p))
        )
    bbuf[c, z] = abuf[own]

    for d in range(8):
        p = (me + d) % 8
        if d > 0:
            start(
                remote(fa.at[own], fa.at[own], s_fa.at[p // 2 * 4 + xh * 2 + p % 2], r_fa.at[own],
                       plane(p))
            )
        start(
            remote(fa.at[own], fa.at[own], s_fa.at[p // 2 * 4 + (1 - xh) * 2 + p % 2], r_fa.at[own],
                   across(p))
        )
    for d in range(1, 8):
        zz = (z + d) % 8
        remote(fb.at[c, z], fb.at[c, zz], s_fb.at[zz], r_fb.at[zz], sibling).wait_recv()
    start(remote(fb.at[c], fb.at[c], s_d.at[1], r_d.at[1], sibling))

    for d in range(1, 8):
        zz = (z + d) % 8
        remote(abuf.at[own], bbuf.at[c, zz], s_b.at[zz], r_b.at[zz], sibling).wait_recv()
    start(remote(bbuf.at[c], bbuf.at[c], s_d.at[2], r_d.at[2], sibling))
    for d in range(1, 16):
        s = (own + d) % 16
        remote(fa.at[own], fa.at[s], s_fa.at[s], r_fa.at[s], sibling).wait_recv()
    remote(fb.at[1 - c], fb.at[1 - c], s_d.at[1], r_d.at[1], sibling).wait_recv()

    def first_slot(i, st):
        p = (me + i + 3) % 8
        return moved(p // 2, st) * 4 + p // 4 * 2 + p % 2

    for i in range(8):
        for st in range(2):
            qa[2 * i + st : 2 * i + st + 1, :] = fa[first_slot(i, st)]
    for cc in range(2):
        for zz in range(8):
            count = qa[...] * fb[cc, zz]
            count = count + swap(count)
            count = count + pltpu.roll(count, 32, 1)
            scale[8 * cc + zz] = 1.0 / jnp.maximum(count, 1.0)

    for d in range(1, 16):
        s = (own + d) % 16
        remote(abuf.at[own], abuf.at[s], s_a.at[s], r_a.at[s], sibling).wait_recv()
    remote(bbuf.at[1 - c], bbuf.at[1 - c], s_d.at[2], r_d.at[2], sibling).wait_recv()

    def second(b, _):
        for s in range(4):
            v = bbuf[b // 8, b % 8, s].astype(jnp.float32)
            bf[b, s, 0] = v
            bf[b, s, 1] = swap(v)
        return 0

    lax.fori_loop(0, 16, second, 0, unroll=2)

    def first(i, _):
        forms = []
        for st in range(2):
            slot = first_slot(i, st)
            for s in range(4):
                v = abuf[slot, s].astype(jnp.float32)
                t = swap(v)
                forms.append((jnp.where(low, v, -t), jnp.where(low, t, v)))

        def pair(b, _):
            acc = [None, None]
            for s in range(4):
                v, t = bf[b, s, 0], bf[b, s, 1]
                for st in range(2):
                    u, w = forms[4 * st + s]
                    term = u * v + w * t
                    acc[st] = term if acc[st] is None else acc[st] + term
            for st in range(2):
                a = 2 * i + st
                at = pl.multiple_of((a * 16 + b) * 16, 16)
                cross[pl.ds(at, 16), :] = acc[st] * scale[b, pl.ds(a, 1), :]
            return 0

        lax.fori_loop(0, 16, pair, 0, unroll=2)
        return 0

    mine = slot_of(me)
    for part in range(2):
        lax.fori_loop(4 * part, 4 * part + 4, first, 0)
        for f in range(16):
            v = cross[pl.ds(2048 * part + f, 128, stride=16), :]
            mat[128 * part : 128 * part + 128, 128 * f : 128 * f + 128] = v.astype(jnp.bfloat16)
        if part == 0:
            table.wait()
        for n, count in CHUNKS:
            lags = jnp.dot(
                mat[128 * part : 128 * part + 128, :],
                inv[:, 128 * n : 128 * (n + count)],
                preferred_element_type=jnp.float32,
            ).astype(jnp.bfloat16)
            for i in range(4):
                for j in range(count):
                    sbuf[4 * part + i, n + j] = lags[
                        32 * i : 32 * i + 32, 128 * j : 128 * j + 128
                    ]
            for k, (at, many) in enumerate(GROUPS):
                if n + count == at + many:
                    for i in range(4 * part, 4 * part + 4):
                        if i != 5:
                            start(
                                remote(sbuf.at[i, pl.ds(at, many)], out_ref.at[mine, pl.ds(at, many)],
                                       s_o.at[k, i], r_o.at[k, mine], plane((me + i + 3) % 8))
                            )
    keep = pltpu.make_async_copy(sbuf.at[5], out_ref.at[mine], tsem)
    keep.start()
    for k, (at, many) in enumerate(GROUPS):
        for d in range(1, 8):
            s = slot_of((me + d) % 8)
            remote(sbuf.at[0, pl.ds(at, many)], out_ref.at[s, pl.ds(at, many)],
                   s_o.at[k, 0], r_o.at[k, s], sibling).wait_recv()
    keep.wait()
    for copy in sent:
        copy.wait_send()


def place(lags_ref, out_ref, rows):
    for n in range(BLOCKS):
        width = min(128, LAGS - 128 * n)
        for a in range(2):
            for s in range(8):
                for st in range(2):
                    at = s // 4 * 64 + s // 2 % 2 * 4 + s % 2 + st * 2
                    v = lags_ref[s, n, 16 * a + 8 * st : 16 * a + 8 * st + 8, :]
                    rows[pl.ds((2 * n + a) * 128 + at, 8, stride=8), :] = v.astype(jnp.float32)
            v = rows[(2 * n + a) * 128 : (2 * n + a + 1) * 128, :]
            out_ref[a, :, 128 * n : 128 * n + width] = v[:, :width]


def on_device(traces, response_re, response_im, station_net, quality):
    twiddle, outer, inverse = tables()
    f32, bf16 = jnp.float32, jnp.bfloat16
    vmem = pl.BlockSpec(memory_space=pltpu.VMEM)
    dma = pltpu.SemaphoreType.DMA
    lags = pl.pallas_call(
        kernel,
        out_shape=jax.ShapeDtypeStruct((8, BLOCKS, 32, 128), bf16),
        in_specs=[pl.BlockSpec(memory_space=pltpu.HBM)] * 8,
        out_specs=pl.BlockSpec(memory_space=pl.ANY),
        scratch_shapes=[
            pltpu.SMEM(station_net.shape, jnp.int32),
            pltpu.SMEM(quality.shape, jnp.int32),
            pltpu.VMEM(traces.shape, f32),
            pltpu.VMEM(response_re.shape, f32),
            pltpu.VMEM(response_im.shape, f32),
            pltpu.VMEM(twiddle.shape, f32),
            pltpu.VMEM(outer.shape, f32),
            pltpu.VMEM((FFT, BLOCKS * 128), bf16),
            pltpu.VMEM((10, 8, 128), f32),
            pltpu.VMEM((128, 256), f32),
            pltpu.VMEM((128, 128), f32),
            pltpu.VMEM((128, 128), f32),
            pltpu.VMEM((2, 40, 128), f32),
            pltpu.VMEM((2, 40, 128), f32),
            pltpu.VMEM((2, 8, 16, 128), f32),
            pltpu.VMEM((8, 8, 128), jnp.int32),
            pltpu.VMEM((8, 16, 128), f32),
            pltpu.VMEM((8, 16, 128), f32),
            pltpu.VMEM((16, 1, 128), f32),
            pltpu.VMEM((2, 8, 1, 128), f32),
            pltpu.VMEM((16, 4, 16, 128), bf16),
            pltpu.VMEM((2, 8, 4, 16, 128), bf16),
            pltpu.VMEM((16, 4, 2, 16, 128), f32),
            pltpu.VMEM((16, 128), f32),
            pltpu.VMEM((16, 16, 128), f32),
            pltpu.VMEM((4096, 128), f32),
            pltpu.VMEM((256, FFT), bf16),
            pltpu.VMEM((8, BLOCKS, 32, 128), bf16),
            dma((7,)), dma, dma((2,)), dma((2,)), dma((8,)), dma((8,)), dma((8,)), dma((8,)),
            dma((3,)), dma((3,)), dma((8,)), dma((8,)), dma((16,)), dma((16,)), dma((8,)), dma((8,)),
            dma((16,)), dma((16,)), dma((8,)), dma((8,)), dma((2, 8)), dma((2, 8)),
        ],
        compiler_params=pltpu.CompilerParams(
            collective_id=0, has_side_effects=True, vmem_limit_bytes=64 << 20
        ),
    )(
        station_net, quality, traces, response_re, response_im,
        jnp.asarray(twiddle), jnp.asarray(outer), jnp.asarray(inverse),
    )
    return pl.pallas_call(
        place,
        out_shape=jax.ShapeDtypeStruct((2, 128, LAGS), f32),
        in_specs=[vmem],
        out_specs=vmem,
        scratch_shapes=[pltpu.VMEM((2 * BLOCKS * 128, 128), f32)],
        compiler_params=pltpu.CompilerParams(vmem_limit_bytes=16 << 20),
    )(lags)


def solution(mesh):
    return jax.shard_map(
        on_device,
        mesh=mesh,
        in_specs=(P("sta", "win"), P("sta", None), P("sta", None), P("sta"), P("sta", "win")),
        out_specs=P("sta", "win", None),
        check_vma=False,
    )
```

time: 47.1 us -> 40.7 us (0.86)
  Pallas kernels: 44.7 us -> 38.3 us
    pallas_call x1, Pallas kernels: 44.5 us -> 38.1 us  [on_device(): pl.pallas_call(kernel, out_shape=jax.ShapeDtypeStruct((8, BLOCKS, 32, 128...]
where the time goes in v3:
time: 40.7 us; the launch traced here: 40.6 us
  Pallas kernels  38.3 us (94%)
  local copies, waits for them, and re-layouts  2.27 us (6%)
    pallas_call x1, Pallas kernels, on_device(): pl.pallas_call(kernel, out_shape=jax.ShapeDtypeStruct((8, BLOCKS, 32, 128...  38.1 us
    pallas_call x1, local copies, waits for them, and re-layouts, on_device(): pl.pallas_call(place, out_shape=jax.ShapeDtypeStruct((2, 128, LAGS), f32)...  1.26 us
    unnamed x2, local copies, waits for them, and re-layouts  1.01 us

profile of v3, /device:TPU:1, one launch (start us, length us, event | category | flops | bytes accessed | tf_op | source)
XLA Modules:
  0.0 40.6 jit_solution(4858530265498882066)
XLA Ops:
  0.0 38.1 %shard_map.82.lags_ref = bf16[8,7,32,128]{3,2,1,0:T(8,128)(2,1)} custom-call(s32[2]{0:T(128)} %net_hbm.1, s32[2,2]{1,0:T(2,128)} %qual_hbm.1, f32[2,2400]{1,0:T(2,128)} %tr_hbm.1, f32[1,1024]{1,0:T(1,128)} %re_hbm.1, f32[1,1024]{1,0:T(1,128)} %im_hbm.1, f32[2,16,128]{2,1,0:T(8,128)} %constant.6.clone.tw_hbm, f32[256,128]{1,0:T(8,128)} %constant.7.clone.outer_hbm, ...), custom_call_target="tpu_custom_call" | custom-call | tf_op jit(solution)/shard_map/pallas_call | solution.py:397
  38.1 0.0 copy-start
  38.1 1.0 %copy-done = bf16[8,7,32,128]{3,2,1,0:T(8,128)(2,1)S(1)} copy-done((bf16[8,7,32,128]{3,2,1,0:T(8,128)(2,1)S(1)}, bf16[8,7,32,128]{3,2,1,0:T(8,128)(2,1)}, u32[]{:S(2)}) %copy-start) | copy-done | bytes 458776
  39.1 0.2 shard_map.83
  39.3 1.3 %copy.9 = f32[2,128,801]{1,0,2:T(2,128)} copy(f32[2,128,801]{2,1,0:T(8,128)S(1)} %shard_map.83) | data formatting | bytes 1640448 | tf_op jit(solution)/shard_map/pallas_call | solution.py:442
Async XLA Ops:
  38.1 1.0 %copy-start = (bf16[8,7,32,128]{3,2,1,0:T(8,128)(2,1)S(1)}, bf16[8,7,32,128]{3,2,1,0:T(8,128)(2,1)}, u32[]{:S(2)}) copy-start(bf16[8,7,32,128]{3,2,1,0:T(8,128)(2,1)} %shard_map.82.lags_ref) | copy-start | bytes 1376260

commit v4 on v3

--- a/solution.py
+++ b/solution.py
@@ -52,8 +52,8 @@
 
 def kernel(
     net_hbm, qual_hbm, tr_hbm, re_hbm, im_hbm, tw_hbm, outer_hbm, inv_hbm, out_ref,
-    net_ref, qual_ref, tr_ref, re_ref, im_ref, tw_ref, outer_ref, inv,
-    xs, lhs, xscr, sq, xsend, xrecv, gbuf, nbuf, csend, crecv, fa, fb, abuf, bbuf, bf, qa, scale, cross, mat, sbuf,
+    net_ref, qual_ref, tr_ref, tw_ref, outer_ref, inv,
+    xs, lhs, xscr, sq, xsend, xrecv, gbuf, nbuf, csend, crecv, fa, fb, abuf, bbuf, rows, af, bf, qa, scale, mat, sbuf,
     isem, tsem, s_x, r_x, s_r1, r_r1, s_n, r_n, s_d, r_d, s_r2, r_r2, s_fa, r_fa, s_fb, r_fb, s_a, r_a, s_b, r_b,
     s_o, r_o,
 ):
@@ -85,18 +85,6 @@
         st = which(p // 2, xh)
         return (moved(p // 2, st) % 2) * 4 + p % 2 * 2 + st
 
-    loads = [
-        pltpu.make_async_copy(src, dst, isem.at[i])
-        for i, (src, dst) in enumerate(
-            (
-                (re_hbm, re_ref), (im_hbm, im_ref), (tr_hbm, tr_ref), (net_hbm, net_ref),
-                (qual_hbm, qual_ref), (tw_hbm, tw_ref), (outer_hbm, outer_ref),
-            )
-        )
-    ]
-    for load in loads:
-        load.start()
-
     barrier = pltpu.get_barrier_semaphore()
 
     def greet(to):
@@ -109,15 +97,23 @@
     greet(device(home, z, xl, c, 0))
     greet(device(home, z, xl, c, 1))
 
+    sq[...] = jnp.zeros((128, 128), jnp.float32)
+    loads = [
+        pltpu.make_async_copy(src, dst, isem.at[i])
+        for i, (src, dst) in enumerate(
+            (
+                (re_hbm, sq.at[pl.ds(0, 8)]), (im_hbm, sq.at[pl.ds(64, 8)]), (net_hbm, net_ref),
+                (tr_hbm, tr_ref), (qual_hbm, qual_ref), (tw_hbm, tw_ref), (outer_hbm, outer_ref),
+            )
+        )
+    ]
+    for load in loads:
+        load.start()
     table = pltpu.make_async_copy(inv_hbm, inv, tsem)
     table.start()
 
-    for load in loads:
+    for load in loads[:2]:
         load.wait()
-    sq[...] = jnp.zeros((128, 128), jnp.float32)
-    for j in range(8):
-        sq[j : j + 1, :] = re_ref[:, 128 * j : 128 * j + 128]
-        sq[64 + j : 65 + j, :] = im_ref[:, 128 * j : 128 * j + 128]
     turned = sq[...].T
     resp = turned[0:16, :]
     for m in range(1, 8):
@@ -126,9 +122,36 @@
     power = square + swap(square)
     level = 0.1 * (jnp.sum(square) / BINS) + 1e-06
     gbuf[c, z] = jnp.where(low, resp, -resp) / (power + level)
-
+    loads[2].wait()
     row = lax.broadcasted_iota(jnp.int32, (8, 128), 0)
     nbuf[me] = jnp.where(row < 4, net_ref[0], net_ref[1])
+
+    pl.semaphore_wait(barrier, 17)
+
+    def remote(src, dst, ssem, rsem, to):
+        return pltpu.make_async_remote_copy(
+            src_ref=src, dst_ref=dst, send_sem=ssem, recv_sem=rsem, device_id=to,
+            device_id_type=MESH,
+        )
+
+    sent = []
+
+    def start(copy):
+        copy.start()
+        sent.append(copy)
+
+    sibling = device(y, z, xl, 1 - c, xh)
+    for d in (4, 3, 5, 2, 6, 1, 7):
+        zz = (z + d) % 8
+        start(
+            remote(gbuf.at[c, z], gbuf.at[c, z], s_r1.at[zz], r_r1.at[z], device(y, zz, xl, c, xh))
+        )
+    for d in range(1, 8):
+        p = (me + d) % 8
+        start(remote(nbuf.at[me], nbuf.at[me], s_n.at[p], r_n.at[me], plane(p)))
+
+    for load in loads[3:]:
+        load.wait()
 
     for q in range(10):
         n = min(128, SEG - 128 * q)
@@ -161,35 +184,11 @@
             flags = jnp.where(group == 2 * xh + g, flag, flags)
         xsend[st, 32:40] = flags
 
-    pl.semaphore_wait(barrier, 17)
-
-    def remote(src, dst, ssem, rsem, to):
-        return pltpu.make_async_remote_copy(
-            src_ref=src, dst_ref=dst, send_sem=ssem, recv_sem=rsem, device_id=to,
-            device_id_type=MESH,
-        )
-
-    sent = []
-
-    def start(copy):
-        copy.start()
-        sent.append(copy)
-
-    sibling = device(y, z, xl, 1 - c, xh)
-    for d in (4, 3, 5, 2, 6, 1, 7):
-        zz = (z + d) % 8
-        start(
-            remote(gbuf.at[c, z], gbuf.at[c, z], s_r1.at[zz], r_r1.at[z],
-                   device(y, zz, xl, c, xh))
-        )
     for st in range(2):
         start(
             remote(xsend.at[st], xrecv.at[xh], s_x.at[st], r_x.at[xh],
                    device(moved(y, st), z, xl, c, y // 2))
         )
-    for d in range(1, 8):
-        p = (me + d) % 8
-        start(remote(nbuf.at[me], nbuf.at[me], s_n.at[p], r_n.at[me], plane(p)))
     for x in range(2):
         remote(xsend.at[0], xrecv.at[x], s_x.at[0], r_x.at[x], sibling).wait_recv()
     mark = xrecv[0, 32:33, :] + xrecv[1, 32:33, :]
@@ -224,7 +223,7 @@
         start(remote(csend.at[p], crecv.at[me], s_r2.at[p], r_r2.at[me], plane(p)))
     factor = choose(me)
     specs = [xrecv[x, 16 * g : 16 * g + 16, :] for x in range(2) for g in range(2)]
-    turned = [swap(spec) for spec in specs]
+    crossed = [swap(spec) for spec in specs]
     for d in range(1, 8):
         p = (me + d) % 8
         remote(csend.at[p], crecv.at[p], s_r2.at[p], r_r2.at[p], plane(p)).wait_recv()
@@ -234,7 +233,7 @@
     f_re = jnp.where(low, factor, turn)
     f_im = jnp.where(low, -turn, factor)
     for s in range(4):
-        dec = specs[s] * f_re + turned[s] * f_im
+        dec = specs[s] * f_re + crossed[s] * f_im
         square = dec * dec
         energy = square + swap(square)
         mean = jnp.sum(square) / BINS + 1e-06
@@ -287,62 +286,58 @@
         p = (me + i + 3) % 8
         return moved(p // 2, st) * 4 + p // 4 * 2 + p % 2
 
+    for cc in range(2):
+        for zz in range(8):
+            qa[8 * cc + zz : 8 * cc + zz + 1, :] = fb[cc, zz]
     for i in range(8):
         for st in range(2):
-            qa[2 * i + st : 2 * i + st + 1, :] = fa[first_slot(i, st)]
-    for cc in range(2):
-        for zz in range(8):
-            count = qa[...] * fb[cc, zz]
+            count = qa[...] * fa[first_slot(i, st)]
             count = count + swap(count)
             count = count + pltpu.roll(count, 32, 1)
-            scale[8 * cc + zz] = 1.0 / jnp.maximum(count, 1.0)
+            scale[2 * i + st] = 1.0 / jnp.maximum(count, 1.0)
 
     for d in range(1, 16):
         s = (own + d) % 16
         remote(abuf.at[own], abuf.at[s], s_a.at[s], r_a.at[s], sibling).wait_recv()
-    remote(bbuf.at[1 - c], bbuf.at[1 - c], s_d.at[2], r_d.at[2], sibling).wait_recv()
-
-    def second(b, _):
-        for s in range(4):
-            v = bbuf[b // 8, b % 8, s].astype(jnp.float32)
-            bf[b, s, 0] = v
-            bf[b, s, 1] = swap(v)
-        return 0
-
-    lax.fori_loop(0, 16, second, 0, unroll=2)
 
     def first(i, _):
-        forms = []
         for st in range(2):
             slot = first_slot(i, st)
             for s in range(4):
                 v = abuf[slot, s].astype(jnp.float32)
                 t = swap(v)
-                forms.append((jnp.where(low, v, -t), jnp.where(low, t, v)))
-
-        def pair(b, _):
-            acc = [None, None]
-            for s in range(4):
-                v, t = bf[b, s, 0], bf[b, s, 1]
-                for st in range(2):
-                    u, w = forms[4 * st + s]
-                    term = u * v + w * t
-                    acc[st] = term if acc[st] is None else acc[st] + term
-            for st in range(2):
-                a = 2 * i + st
-                at = pl.multiple_of((a * 16 + b) * 16, 16)
-                cross[pl.ds(at, 16), :] = acc[st] * scale[b, pl.ds(a, 1), :]
-            return 0
-
-        lax.fori_loop(0, 16, pair, 0, unroll=2)
+                af[2 * i + st, s, 0] = jnp.where(low, v, -t)
+                af[2 * i + st, s, 1] = jnp.where(low, t, v)
         return 0
+
+    lax.fori_loop(0, 8, first, 0)
+    remote(bbuf.at[1 - c], bbuf.at[1 - c], s_d.at[2], r_d.at[2], sibling).wait_recv()
+
+    for b in range(16):
+        for s in range(4):
+            rows[s, 16 * b : 16 * b + 16, :] = bbuf[b // 8, b % 8, s].astype(jnp.float32)
+    for s in range(4):
+        for f in range(16):
+            v = rows[s, pl.ds(f, 16, stride=16), :]
+            bf[f, s, 0] = v
+            bf[f, s, 1] = swap(v)
 
     mine = slot_of(me)
     for part in range(2):
-        lax.fori_loop(4 * part, 4 * part + 4, first, 0)
-        for f in range(16):
-            v = cross[pl.ds(2048 * part + f, 128, stride=16), :]
-            mat[128 * part : 128 * part + 128, 128 * f : 128 * f + 128] = v.astype(jnp.bfloat16)
+
+        def pairs(f, _, part=part):
+            other = [(bf[f, s, 0], bf[f, s, 1]) for s in range(4)]
+            at = pl.multiple_of(128 * f, 128)
+            for a in range(8 * part, 8 * part + 8):
+                acc = None
+                for s in range(4):
+                    term = af[a, s, 0, pl.ds(f, 1), :] * other[s][0]
+                    term = term + af[a, s, 1, pl.ds(f, 1), :] * other[s][1]
+                    acc = term if acc is None else acc + term
+                mat[16 * a : 16 * a + 16, pl.ds(at, 128)] = (acc * scale[a]).astype(jnp.bfloat16)
+            return 0
+
+        lax.fori_loop(0, 16, pairs, 0)
         if part == 0:
             table.wait()
         for n, count in CHUNKS:
@@ -376,7 +371,8 @@
         copy.wait_send()
 
 
-def place(lags_ref, out_ref, rows):
+def place(lags_ref, out_ref, rows, stage, sem):
+    copies = []
     for n in range(BLOCKS):
         width = min(128, LAGS - 128 * n)
         for a in range(2):
@@ -384,9 +380,13 @@
                 for st in range(2):
                     at = s // 4 * 64 + s // 2 % 2 * 4 + s % 2 + st * 2
                     v = lags_ref[s, n, 16 * a + 8 * st : 16 * a + 8 * st + 8, :]
-                    rows[pl.ds((2 * n + a) * 128 + at, 8, stride=8), :] = v.astype(jnp.float32)
-            v = rows[(2 * n + a) * 128 : (2 * n + a + 1) * 128, :]
-            out_ref[a, :, 128 * n : 128 * n + width] = v[:, :width]
+                    rows[2 * n + a, pl.ds(at, 8, stride=8), :] = v.astype(jnp.float32)
+            stage[128 * n : 128 * n + 128, a, :] = rows[2 * n + a].T
+        part = pl.ds(128 * n, width)
+        copies.append(pltpu.make_async_copy(stage.at[part], out_ref.at[part], sem.at[n]))
+        copies[-1].start()
+    for copy in copies:
+        copy.wait()
 
 
 def on_device(traces, response_re, response_im, station_net, quality):
@@ -403,8 +403,6 @@
             pltpu.SMEM(station_net.shape, jnp.int32),
             pltpu.SMEM(quality.shape, jnp.int32),
             pltpu.VMEM(traces.shape, f32),
-            pltpu.VMEM(response_re.shape, f32),
-            pltpu.VMEM(response_im.shape, f32),
             pltpu.VMEM(twiddle.shape, f32),
             pltpu.VMEM(outer.shape, f32),
             pltpu.VMEM((FFT, BLOCKS * 128), bf16),
@@ -422,10 +420,11 @@
             pltpu.VMEM((2, 8, 1, 128), f32),
             pltpu.VMEM((16, 4, 16, 128), bf16),
             pltpu.VMEM((2, 8, 4, 16, 128), bf16),
+            pltpu.VMEM((4, 256, 128), f32),
+            pltpu.VMEM((16, 4, 2, 16, 128), f32),
             pltpu.VMEM((16, 4, 2, 16, 128), f32),
             pltpu.VMEM((16, 128), f32),
             pltpu.VMEM((16, 16, 128), f32),
-            pltpu.VMEM((4096, 128), f32),
             pltpu.VMEM((256, FFT), bf16),
             pltpu.VMEM((8, BLOCKS, 32, 128), bf16),
             dma((7,)), dma, dma((2,)), dma((2,)), dma((8,)), dma((8,)), dma((8,)), dma((8,)),
@@ -433,20 +432,31 @@
             dma((16,)), dma((16,)), dma((8,)), dma((8,)), dma((2, 8)), dma((2, 8)),
         ],
         compiler_params=pltpu.CompilerParams(
-            collective_id=0, has_side_effects=True, vmem_limit_bytes=64 << 20
+            collective_id=0, has_side_effects=True, vmem_limit_bytes=40 << 20
         ),
     )(
-        station_net, quality, traces, response_re, response_im,
-        jnp.asarray(twiddle), jnp.asarray(outer), jnp.asarray(inverse),
+        *(
+            pltpu.with_memory_space_constraint(v, pltpu.HBM)
+            for v in (
+                station_net, quality, traces, response_re.reshape(8, 128),
+                response_im.reshape(8, 128), jnp.asarray(twiddle), jnp.asarray(outer),
+                jnp.asarray(inverse),
+            )
+        )
     )
-    return pl.pallas_call(
+    placed = pl.pallas_call(
         place,
-        out_shape=jax.ShapeDtypeStruct((2, 128, LAGS), f32),
+        out_shape=jax.ShapeDtypeStruct((LAGS, 2, 128), f32),
         in_specs=[vmem],
-        out_specs=vmem,
-        scratch_shapes=[pltpu.VMEM((2 * BLOCKS * 128, 128), f32)],
+        out_specs=pl.BlockSpec(memory_space=pl.ANY),
+        scratch_shapes=[
+            pltpu.VMEM((2 * BLOCKS, 128, 128), f32),
+            pltpu.VMEM((128 * BLOCKS, 2, 128), f32),
+            dma((BLOCKS,)),
+        ],
         compiler_params=pltpu.CompilerParams(vmem_limit_bytes=16 << 20),
     )(lags)
+    return placed.transpose(1, 2, 0)
 
 
 def solution(mesh):

time: 40.7 us -> 39.5 us (0.971)
  local copies, waits for them, and re-layouts: 2.27 us -> 0 us
  Pallas kernels: 38.3 us -> 39.4 us
    pallas_call x1, Pallas kernels: 0.19 us -> 1.55 us  [on_device(): pl.pallas_call(place, out_shape=jax.ShapeDtypeStruct((LAGS, 2, 128), f32)...]
    pallas_call x1 -> x0, local copies, waits for them, and re-layouts: 1.26 us -> none  [on_device(): pl.pallas_call(place, out_shape=jax.ShapeDtypeStruct((2, 128, LAGS), f32)...]
    unnamed x2 -> x0, local copies, waits for them, and re-layouts: 1.01 us -> none
where the time goes in v4:
time: 39.5 us; the launch traced here: 39.4 us
  Pallas kernels  39.4 us (100%)
    pallas_call x1, Pallas kernels, on_device(): pl.pallas_call(kernel, out_shape=jax.ShapeDtypeStruct((8, BLOCKS, 32, 128...  37.9 us
    pallas_call x1, Pallas kernels, on_device(): pl.pallas_call(place, out_shape=jax.ShapeDtypeStruct((LAGS, 2, 128), f32)...  1.55 us

profile of v4, /device:TPU:1, one launch (start us, length us, event | category | flops | bytes accessed | tf_op | source)
XLA Modules:
  0.0 39.4 jit_solution(15895553537117526347)
XLA Ops:
  0.0 37.9 %shard_map.82.lags_ref = bf16[8,7,32,128]{3,2,1,0:T(8,128)(2,1)S(1)} custom-call(s32[2]{0:T(128)} %net_hbm.1, s32[2,2]{1,0:T(2,128)} %qual_hbm.1, f32[2,2400]{1,0:T(2,128)} %tr_hbm.1, f32[8,128]{1,0:T(8,128)} %bitcast.3, f32[8,128]{1,0:T(8,128)} %bitcast.4, f32[2,16,128]{2,1,0:T(8,128)} %constant.6.clone.tw_hbm, f32[256,128]{1,0:T(8,128)} %constant.7.clone.outer_hbm, ...), custom_call_target="tpu_custom_call" | custom-call | tf_op jit(solution)/shard_map/pallas_call | solution.py:397
  37.9 1.5 %shard_map.83 = f32[801,2,128]{2,1,0:T(2,128)} custom-call(bf16[8,7,32,128]{3,2,1,0:T(8,128)(2,1)S(1)} %shard_map.82.lags_ref), custom_call_target="tpu_custom_call" | custom-call | tf_op jit(solution)/shard_map/pallas_call | solution.py:447

commit v5 on v4

--- a/solution.py
+++ b/solution.py
@@ -15,7 +15,8 @@
 LAGS = 2 * MAXLAG + 1
 BLOCKS = 7
 CHUNKS = ((0, 2), (2, 2), (4, 2), (6, 1))
-GROUPS = ((0, 4), (4, 3))
+GROUPS = ((0, 4), (4, 2), (6, 1))
+PARTS = ((0, 4), (4, 8))
 HIGHEST = lax.Precision.HIGHEST
 
 
@@ -53,7 +54,7 @@
 def kernel(
     net_hbm, qual_hbm, tr_hbm, re_hbm, im_hbm, tw_hbm, outer_hbm, inv_hbm, out_ref,
     net_ref, qual_ref, tr_ref, tw_ref, outer_ref, inv,
-    xs, lhs, xscr, sq, xsend, xrecv, gbuf, nbuf, csend, crecv, fa, fb, abuf, bbuf, rows, af, bf, qa, scale, mat, sbuf,
+    xs, lhs, xscr, sq, xsend, xrecv, gbuf, nbuf, csend, crecv, fa, fb, abuf, bbuf, rows, af, bf, qa, scale, mat, sbuf, rbuf, turn_buf,
     isem, tsem, s_x, r_x, s_r1, r_r1, s_n, r_n, s_d, r_d, s_r2, r_r2, s_fa, r_fa, s_fb, r_fb, s_a, r_a, s_b, r_b,
     s_o, r_o,
 ):
@@ -323,12 +324,12 @@
             bf[f, s, 1] = swap(v)
 
     mine = slot_of(me)
-    for part in range(2):
-
-        def pairs(f, _, part=part):
+    for lo, hi in PARTS:
+
+        def pairs(f, _, lo=lo, hi=hi):
             other = [(bf[f, s, 0], bf[f, s, 1]) for s in range(4)]
             at = pl.multiple_of(128 * f, 128)
-            for a in range(8 * part, 8 * part + 8):
+            for a in range(2 * lo, 2 * hi):
                 acc = None
                 for s in range(4):
                     term = af[a, s, 0, pl.ds(f, 1), :] * other[s][0]
@@ -338,67 +339,55 @@
             return 0
 
         lax.fori_loop(0, 16, pairs, 0)
-        if part == 0:
+        if lo == 0:
             table.wait()
         for n, count in CHUNKS:
             lags = jnp.dot(
-                mat[128 * part : 128 * part + 128, :],
+                mat[32 * lo : 32 * hi, :],
                 inv[:, 128 * n : 128 * (n + count)],
                 preferred_element_type=jnp.float32,
             ).astype(jnp.bfloat16)
-            for i in range(4):
+            for i in range(hi - lo):
                 for j in range(count):
-                    sbuf[4 * part + i, n + j] = lags[
-                        32 * i : 32 * i + 32, 128 * j : 128 * j + 128
-                    ]
+                    sbuf[lo + i, n + j] = lags[32 * i : 32 * i + 32, 128 * j : 128 * j + 128]
             for k, (at, many) in enumerate(GROUPS):
                 if n + count == at + many:
-                    for i in range(4 * part, 4 * part + 4):
+                    for i in range(lo, hi):
                         if i != 5:
                             start(
-                                remote(sbuf.at[i, pl.ds(at, many)], out_ref.at[mine, pl.ds(at, many)],
+                                remote(sbuf.at[i, pl.ds(at, many)], rbuf.at[mine, pl.ds(at, many)],
                                        s_o.at[k, i], r_o.at[k, mine], plane((me + i + 3) % 8))
                             )
-    keep = pltpu.make_async_copy(sbuf.at[5], out_ref.at[mine], tsem)
+    keep = pltpu.make_async_copy(sbuf.at[5], rbuf.at[mine], tsem)
     keep.start()
+    keep.wait()
     for k, (at, many) in enumerate(GROUPS):
         for d in range(1, 8):
             s = slot_of((me + d) % 8)
-            remote(sbuf.at[0, pl.ds(at, many)], out_ref.at[s, pl.ds(at, many)],
+            remote(sbuf.at[0, pl.ds(at, many)], rbuf.at[s, pl.ds(at, many)],
                    s_o.at[k, 0], r_o.at[k, s], sibling).wait_recv()
-    keep.wait()
+        for n in range(at, at + many):
+            width = min(128, LAGS - 128 * n)
+            for a in range(2):
+                for s in range(8):
+                    for st in range(2):
+                        to = s // 4 * 64 + s // 2 % 2 * 4 + s % 2 + st * 2
+                        v = rbuf[s, n, 16 * a + 8 * st : 16 * a + 8 * st + 8, :]
+                        turn_buf[2 * n + a, pl.ds(to, 8, stride=8), :] = v.astype(jnp.float32)
+                out_ref[128 * n : 128 * n + width, a, :] = turn_buf[2 * n + a].T[:width]
     for copy in sent:
         copy.wait_send()
-
-
-def place(lags_ref, out_ref, rows, stage, sem):
-    copies = []
-    for n in range(BLOCKS):
-        width = min(128, LAGS - 128 * n)
-        for a in range(2):
-            for s in range(8):
-                for st in range(2):
-                    at = s // 4 * 64 + s // 2 % 2 * 4 + s % 2 + st * 2
-                    v = lags_ref[s, n, 16 * a + 8 * st : 16 * a + 8 * st + 8, :]
-                    rows[2 * n + a, pl.ds(at, 8, stride=8), :] = v.astype(jnp.float32)
-            stage[128 * n : 128 * n + 128, a, :] = rows[2 * n + a].T
-        part = pl.ds(128 * n, width)
-        copies.append(pltpu.make_async_copy(stage.at[part], out_ref.at[part], sem.at[n]))
-        copies[-1].start()
-    for copy in copies:
-        copy.wait()
 
 
 def on_device(traces, response_re, response_im, station_net, quality):
     twiddle, outer, inverse = tables()
     f32, bf16 = jnp.float32, jnp.bfloat16
-    vmem = pl.BlockSpec(memory_space=pltpu.VMEM)
     dma = pltpu.SemaphoreType.DMA
     lags = pl.pallas_call(
         kernel,
-        out_shape=jax.ShapeDtypeStruct((8, BLOCKS, 32, 128), bf16),
+        out_shape=jax.ShapeDtypeStruct((LAGS, 2, 128), f32),
         in_specs=[pl.BlockSpec(memory_space=pltpu.HBM)] * 8,
-        out_specs=pl.BlockSpec(memory_space=pl.ANY),
+        out_specs=pl.BlockSpec(memory_space=pltpu.VMEM),
         scratch_shapes=[
             pltpu.SMEM(station_net.shape, jnp.int32),
             pltpu.SMEM(quality.shape, jnp.int32),
@@ -427,9 +416,11 @@
             pltpu.VMEM((16, 16, 128), f32),
             pltpu.VMEM((256, FFT), bf16),
             pltpu.VMEM((8, BLOCKS, 32, 128), bf16),
+            pltpu.VMEM((8, BLOCKS, 32, 128), bf16),
+            pltpu.VMEM((2 * BLOCKS, 128, 128), f32),
             dma((7,)), dma, dma((2,)), dma((2,)), dma((8,)), dma((8,)), dma((8,)), dma((8,)),
             dma((3,)), dma((3,)), dma((8,)), dma((8,)), dma((16,)), dma((16,)), dma((8,)), dma((8,)),
-            dma((16,)), dma((16,)), dma((8,)), dma((8,)), dma((2, 8)), dma((2, 8)),
+            dma((16,)), dma((16,)), dma((8,)), dma((8,)), dma((4, 8)), dma((4, 8)),
         ],
         compiler_params=pltpu.CompilerParams(
             collective_id=0, has_side_effects=True, vmem_limit_bytes=40 << 20
@@ -444,19 +435,7 @@
             )
         )
     )
-    placed = pl.pallas_call(
-        place,
-        out_shape=jax.ShapeDtypeStruct((LAGS, 2, 128), f32),
-        in_specs=[vmem],
-        out_specs=pl.BlockSpec(memory_space=pl.ANY),
-        scratch_shapes=[
-            pltpu.VMEM((2 * BLOCKS, 128, 128), f32),
-            pltpu.VMEM((128 * BLOCKS, 2, 128), f32),
-            dma((BLOCKS,)),
-        ],
-        compiler_params=pltpu.CompilerParams(vmem_limit_bytes=16 << 20),
-    )(lags)
-    return placed.transpose(1, 2, 0)
+    return lags.transpose(1, 2, 0)
 
 
 def solution(mesh):

time: 39.5 us -> 38.7 us (0.980)
  Pallas kernels: 39.4 us -> 37.7 us
  local copies, waits for them, and re-layouts: 0 us -> 0.89 us
    pallas_call x2 -> x1, Pallas kernels: 39.4 us -> 37.7 us  [on_device(): pl.pallas_call(kernel, out_shape=jax.ShapeDtypeStruct((LAGS, 2, 128), f32...]
    unnamed x0 -> x1, local copies, waits for them, and re-layouts: none -> 0.89 us
where the time goes in v5:
time: 38.7 us; the launch traced here: 38.6 us
  Pallas kernels  37.7 us (97%)
  local copies, waits for them, and re-layouts  0.89 us (2%)
    pallas_call x1, Pallas kernels, on_device(): pl.pallas_call(kernel, out_shape=jax.ShapeDtypeStruct((LAGS, 2, 128), f32...  37.7 us
    unnamed x1, local copies, waits for them, and re-layouts  0.89 us

profile of v5, /device:TPU:1, one launch (start us, length us, event | category | flops | bytes accessed | tf_op | source)
XLA Modules:
  0.0 38.6 jit_solution(1517824819171667503)
XLA Ops:
  0.0 37.7 %shard_map.82 = f32[801,2,128]{2,1,0:T(2,128)S(1)} custom-call(s32[2]{0:T(128)} %net_hbm.1, s32[2,2]{1,0:T(2,128)} %qual_hbm.1, f32[2,2400]{1,0:T(2,128)} %tr_hbm.1, f32[8,128]{1,0:T(8,128)} %bitcast.4, f32[8,128]{1,0:T(8,128)} %bitcast.5, f32[2,16,128]{2,1,0:T(8,128)} %constant.6.clone.tw_hbm, f32[256,128]{1,0:T(8,128)} %constant.7.clone.outer_hbm, ...), custom_call_target="tpu_custom_call" | custom-call | tf_op jit(solution)/shard_map/pallas_call | solution.py:386
  37.7 0.9 %copy.10 = f32[2,128,801]{1,0,2:T(2,128)} copy(f32[2,128,801]{1,0,2:T(2,128)S(1)} %bitcast.3) | data formatting | bytes 1640448

commit v6 on v5

--- a/solution.py
+++ b/solution.py
@@ -13,10 +13,9 @@
 SEG, BINS, MAXLAG = 1200, 1024, 400
 FFT = 2 * BINS
 LAGS = 2 * MAXLAG + 1
-BLOCKS = 7
-CHUNKS = ((0, 2), (2, 2), (4, 2), (6, 1))
-GROUPS = ((0, 4), (4, 2), (6, 1))
-PARTS = ((0, 4), (4, 8))
+ROWS = 208
+CHUNKS = ((0, 0, 128), (256, 128, 80))
+PARTS = ((0, 2), (2, 4), (4, 6), (6, 8))
 HIGHEST = lax.Precision.HIGHEST
 
 
@@ -32,14 +31,12 @@
     outer = np.concatenate(
         [np.concatenate([c, -s], 1), np.concatenate([s, c], 1)], 0
     ).astype(np.float32)
-    f = f1[:, None] + 16 * f2[None, :]
-    k = np.arange(LAGS) - MAXLAG
-    ang = 2 * np.pi * (f[:, :, None] * k % FFT) / FFT
-    w = np.where(f == 0, 1.0, 2.0)[:, :, None] / math.sqrt(BINS)
-    inverse = np.zeros((16, 128, BLOCKS * 128), np.float64)
-    inverse[:, :64, :LAGS] = w * np.cos(ang)
-    inverse[:, 64:, :LAGS] = -w * np.sin(ang)
-    return twiddle, outer, inverse.reshape(FFT, BLOCKS * 128).astype(ml_dtypes.bfloat16)
+    f = np.concatenate([f1[:8, None] + 16 * f2, f1[8:, None] + 16 * f2], 1).reshape(BINS)
+    k = np.concatenate([np.arange(384), np.tile(384 + np.arange(32), 4)])
+    ang = 2 * np.pi * (f[:, None] * k % FFT) / FFT
+    w = np.where(f == 0, 1.0, 2.0)[:, None] / math.sqrt(BINS)
+    inverse = np.stack([w * np.cos(ang), w * np.sin(ang)]).astype(ml_dtypes.bfloat16)
+    return twiddle, outer, inverse
 
 
 def coords():
@@ -238,7 +235,14 @@
         square = dec * dec
         energy = square + swap(square)
         mean = jnp.sum(square) / BINS + 1e-06
-        abuf[own, s] = (dec / jnp.sqrt(energy + 0.5 * mean)).astype(jnp.bfloat16)
+        white = dec / jnp.sqrt(energy + 0.5 * mean)
+        turn = swap(white)
+        abuf[own, s] = jnp.concatenate(
+            [
+                jnp.where(low[0:8], white[0:8], turn[8:16]),
+                jnp.where(low[0:8], turn[0:8], white[8:16]),
+            ]
+        ).astype(jnp.bfloat16)
 
     for d in (4, 3, 5, 2, 6, 1, 7):
         zz = (z + d) % 8
@@ -301,14 +305,11 @@
         s = (own + d) % 16
         remote(abuf.at[own], abuf.at[s], s_a.at[s], r_a.at[s], sibling).wait_recv()
 
+
     def first(i, _):
         for st in range(2):
-            slot = first_slot(i, st)
             for s in range(4):
-                v = abuf[slot, s].astype(jnp.float32)
-                t = swap(v)
-                af[2 * i + st, s, 0] = jnp.where(low, v, -t)
-                af[2 * i + st, s, 1] = jnp.where(low, t, v)
+                af[2 * i + st, s] = abuf[first_slot(i, st), s].astype(jnp.float32)
         return 0
 
     lax.fori_loop(0, 8, first, 0)
@@ -318,63 +319,99 @@
         for s in range(4):
             rows[s, 16 * b : 16 * b + 16, :] = bbuf[b // 8, b % 8, s].astype(jnp.float32)
     for s in range(4):
-        for f in range(16):
-            v = rows[s, pl.ds(f, 16, stride=16), :]
-            bf[f, s, 0] = v
-            bf[f, s, 1] = swap(v)
+        for r in range(8):
+            bf[r, s, 0] = rows[s, pl.ds(r, 16, stride=16), :]
+            bf[r, s, 1] = rows[s, pl.ds(r + 8, 16, stride=16), :]
 
     mine = slot_of(me)
     for lo, hi in PARTS:
 
-        def pairs(f, _, lo=lo, hi=hi):
-            other = [(bf[f, s, 0], bf[f, s, 1]) for s in range(4)]
-            at = pl.multiple_of(128 * f, 128)
+        def pairs(r, _, lo=lo, hi=hi):
+            other = [(bf[r, s, 0], bf[r, s, 1]) for s in range(4)]
+            at = pl.ds(pl.multiple_of(128 * r, 128), 128)
             for a in range(2 * lo, 2 * hi):
-                acc = None
+                re, im = None, None
                 for s in range(4):
-                    term = af[a, s, 0, pl.ds(f, 1), :] * other[s][0]
-                    term = term + af[a, s, 1, pl.ds(f, 1), :] * other[s][1]
-                    acc = term if acc is None else acc + term
-                mat[16 * a : 16 * a + 16, pl.ds(at, 128)] = (acc * scale[a]).astype(jnp.bfloat16)
+                    u, v = af[a, s, pl.ds(r, 1), :], af[a, s, pl.ds(r + 8, 1), :]
+                    x, w = other[s]
+                    term, turn = u * x + v * w, v * x - u * w
+                    re, im = (term, turn) if re is None else (re + term, im + turn)
+                to = slice(16 * a, 16 * a + 16)
+                mat[0, to, at] = (re * scale[a]).astype(jnp.bfloat16)
+                mat[1, to, at] = (im * scale[a]).astype(jnp.bfloat16)
             return 0
 
-        lax.fori_loop(0, 16, pairs, 0)
+        lax.fori_loop(0, 8, pairs, 0)
         if lo == 0:
             table.wait()
-        for n, count in CHUNKS:
-            lags = jnp.dot(
-                mat[32 * lo : 32 * hi, :],
-                inv[:, 128 * n : 128 * (n + count)],
-                preferred_element_type=jnp.float32,
-            ).astype(jnp.bfloat16)
-            for i in range(hi - lo):
-                for j in range(count):
-                    sbuf[lo + i, n + j] = lags[32 * i : 32 * i + 32, 128 * j : 128 * j + 128]
-            for k, (at, many) in enumerate(GROUPS):
-                if n + count == at + many:
-                    for i in range(lo, hi):
-                        if i != 5:
-                            start(
-                                remote(sbuf.at[i, pl.ds(at, many)], rbuf.at[mine, pl.ds(at, many)],
-                                       s_o.at[k, i], r_o.at[k, mine], plane((me + i + 3) % 8))
-                            )
+        part = slice(32 * lo, 32 * hi)
+        for k, (col, at, many) in enumerate(CHUNKS):
+            even, odd = [
+                jnp.dot(
+                    mat[i, part, :], inv[i, :, col : col + 256], preferred_element_type=jnp.float32
+                )
+                for i in range(2)
+            ]
+            ahead = (even - odd).astype(jnp.bfloat16)
+            back = (even + odd).astype(jnp.bfloat16)
+            for i in range(lo, hi):
+                to = slice(32 * (i - lo), 32 * (i - lo) + 32)
+                if k == 0:
+                    sbuf[i, 0:32], sbuf[i, 32:64] = ahead[to, 0:128], ahead[to, 128:256]
+                    sbuf[i, 64:96], sbuf[i, 96:128] = back[to, 0:128], back[to, 128:256]
+                else:
+                    sbuf[i, 128:160], sbuf[i, 160:192] = ahead[to, 0:128], back[to, 0:128]
+                    ends = jnp.where(
+                        lax.broadcasted_iota(jnp.int32, (32, 128), 1) // 32 % 2 == 0,
+                        ahead[to, 128:256].astype(jnp.float32),
+                        back[to, 128:256].astype(jnp.float32),
+                    )
+                    sbuf[i, 192:208] = jnp.where(low, ends[0:16], ends[16:32]).astype(jnp.bfloat16)
+                if i != 5:
+                    start(
+                        remote(sbuf.at[i, pl.ds(at, many)], rbuf.at[mine, pl.ds(at, many)],
+                               s_o.at[k, i], r_o.at[k, mine], plane((me + i + 3) % 8))
+                    )
     keep = pltpu.make_async_copy(sbuf.at[5], rbuf.at[mine], tsem)
     keep.start()
     keep.wait()
-    for k, (at, many) in enumerate(GROUPS):
+    q, lane = [lax.broadcasted_iota(jnp.int32, (128, 128), i) for i in range(2)]
+    ends = q // 64 * 64 + jnp.where(q % 64 < 32, 48 - q % 64, q % 64 - 32)
+    ahead, back, ends = [
+        jnp.where(lane == to, 1.0, 0.0).astype(jnp.bfloat16) for to in (q, 127 - q, ends)
+    ]
+
+    def turned_block(n, at, order):
+        for s in range(8):
+            for cc in range(2):
+                to = s // 4 * 64 + s // 2 % 2 * 4 + s % 2 + cc * 2
+                v = rbuf[s, at + 8 * cc : at + 8 * cc + 8, :]
+                turn_buf[n, pl.ds(to, 8, stride=8), :] = v.astype(jnp.float32)
+        return lax.dot_general(
+            order, turn_buf[n].astype(jnp.bfloat16), (((1,), (1,)), ((), ())),
+            preferred_element_type=jnp.float32,
+        )
+
+    for k, (_, at, many) in enumerate(CHUNKS):
         for d in range(1, 8):
             s = slot_of((me + d) % 8)
             remote(sbuf.at[0, pl.ds(at, many)], rbuf.at[s, pl.ds(at, many)],
                    s_o.at[k, 0], r_o.at[k, s], sibling).wait_recv()
-        for n in range(at, at + many):
-            width = min(128, LAGS - 128 * n)
+        for a in range(2):
+            for n in (0, 1) if k == 0 else (2,):
+                to = MAXLAG - 128 * n
+                out_ref[to - 127 : to + 1, a, :] = turned_block(
+                    4 * n + 2 * a, (64, 96, 160)[n] + 16 * a, back
+                )
+                to = MAXLAG + 128 * n
+                out_ref[to : to + 128, a, :] = turned_block(
+                    4 * n + 2 * a + 1, (0, 32, 128)[n] + 16 * a, ahead
+                )
+        if k == 1:
+            v = turned_block(12, 192, ends)
             for a in range(2):
-                for s in range(8):
-                    for st in range(2):
-                        to = s // 4 * 64 + s // 2 % 2 * 4 + s % 2 + st * 2
-                        v = rbuf[s, n, 16 * a + 8 * st : 16 * a + 8 * st + 8, :]
-                        turn_buf[2 * n + a, pl.ds(to, 8, stride=8), :] = v.astype(jnp.float32)
-                out_ref[128 * n : 128 * n + width, a, :] = turn_buf[2 * n + a].T[:width]
+                out_ref[0:17, a, :] = v[64 * a : 64 * a + 17]
+                out_ref[784:801, a, :] = v[64 * a + 32 : 64 * a + 49]
     for copy in sent:
         copy.wait_send()
 
@@ -394,7 +431,7 @@
             pltpu.VMEM(traces.shape, f32),
             pltpu.VMEM(twiddle.shape, f32),
             pltpu.VMEM(outer.shape, f32),
-            pltpu.VMEM((FFT, BLOCKS * 128), bf16),
+            pltpu.VMEM(inverse.shape, bf16),
             pltpu.VMEM((10, 8, 128), f32),
             pltpu.VMEM((128, 256), f32),
             pltpu.VMEM((128, 128), f32),
@@ -410,17 +447,17 @@
             pltpu.VMEM((16, 4, 16, 128), bf16),
             pltpu.VMEM((2, 8, 4, 16, 128), bf16),
             pltpu.VMEM((4, 256, 128), f32),
-            pltpu.VMEM((16, 4, 2, 16, 128), f32),
-            pltpu.VMEM((16, 4, 2, 16, 128), f32),
+            pltpu.VMEM((16, 4, 16, 128), f32),
+            pltpu.VMEM((8, 4, 2, 16, 128), f32),
             pltpu.VMEM((16, 128), f32),
             pltpu.VMEM((16, 16, 128), f32),
-            pltpu.VMEM((256, FFT), bf16),
-            pltpu.VMEM((8, BLOCKS, 32, 128), bf16),
-            pltpu.VMEM((8, BLOCKS, 32, 128), bf16),
-            pltpu.VMEM((2 * BLOCKS, 128, 128), f32),
+            pltpu.VMEM((2, 256, BINS), bf16),
+            pltpu.VMEM((8, ROWS, 128), bf16),
+            pltpu.VMEM((8, ROWS, 128), bf16),
+            pltpu.VMEM((13, 128, 128), f32),
             dma((7,)), dma, dma((2,)), dma((2,)), dma((8,)), dma((8,)), dma((8,)), dma((8,)),
             dma((3,)), dma((3,)), dma((8,)), dma((8,)), dma((16,)), dma((16,)), dma((8,)), dma((8,)),
-            dma((16,)), dma((16,)), dma((8,)), dma((8,)), dma((4, 8)), dma((4, 8)),
+            dma((16,)), dma((16,)), dma((8,)), dma((8,)), dma((2, 8)), dma((2, 8)),
         ],
         compiler_params=pltpu.CompilerParams(
             collective_id=0, has_side_effects=True, vmem_limit_bytes=40 << 20

time: 38.7 us -> 37.8 us (0.977)
  Pallas kernels: 37.7 us -> 36.8 us
    pallas_call x1, Pallas kernels: 37.7 us -> 36.8 us  [on_device(): pl.pallas_call(kernel, out_shape=jax.ShapeDtypeStruct((LAGS, 2, 128), f32...]
where the time goes in v6:
time: 37.8 us; the launch traced here: 37.7 us
  Pallas kernels  36.8 us (97%)
  local copies, waits for them, and re-layouts  0.89 us (2%)
    pallas_call x1, Pallas kernels, on_device(): pl.pallas_call(kernel, out_shape=jax.ShapeDtypeStruct((LAGS, 2, 128), f32...  36.8 us
    unnamed x1, local copies, waits for them, and re-layouts  0.89 us

profile of v6, /device:TPU:1, one launch (start us, length us, event | category | flops | bytes accessed | tf_op | source)
XLA Modules:
  0.0 37.7 jit_solution(2917891053473635099)
XLA Ops:
  0.0 36.8 %shard_map.82 = f32[801,2,128]{2,1,0:T(2,128)S(1)} custom-call(s32[2]{0:T(128)} %net_hbm.1, s32[2,2]{1,0:T(2,128)} %qual_hbm.1, f32[2,2400]{1,0:T(2,128)} %tr_hbm.1, f32[8,128]{1,0:T(8,128)} %bitcast.4, f32[8,128]{1,0:T(8,128)} %bitcast.5, f32[2,16,128]{2,1,0:T(8,128)} %constant.6.clone.tw_hbm, f32[256,128]{1,0:T(8,128)} %constant.7.clone.outer_hbm, ...), custom_call_target="tpu_custom_call" | custom-call | tf_op jit(solution)/shard_map/pallas_call | solution.py:423
  36.8 0.9 %copy.10 = f32[2,128,801]{1,0,2:T(2,128)} copy(f32[2,128,801]{1,0,2:T(2,128)S(1)} %bitcast.3) | data formatting | bytes 1640448

commit v7 on v6

--- a/solution.py
+++ b/solution.py
@@ -88,12 +88,13 @@
     def greet(to):
         pl.semaphore_signal(barrier, inc=1, device_id=to, device_id_type=MESH)
 
-    for d in range(1, 8):
+    for d in (4, 3, 5, 2, 6, 1, 7):
         greet(device(y, (z + d) % 8, xl, c, xh))
+    greet(device(home, z, xl, c, 0))
+    greet(device(home, z, xl, c, 1))
+    for d in (4, 5, 3, 2, 6, 1, 7):
         greet(plane((me + d) % 8))
     greet(device(y, z, xl, 1 - c, xh))
-    greet(device(home, z, xl, c, 0))
-    greet(device(home, z, xl, c, 1))
 
     sq[...] = jnp.zeros((128, 128), jnp.float32)
     loads = [
@@ -170,7 +171,7 @@
             tr, ti = tw_ref[0, g : g + 1, :], tw_ref[1, g : g + 1, :]
             lhs[8 * g : 8 * g + 8, 0:128] = ar * tr - ai * ti
             lhs[8 * g : 8 * g + 8, 128:256] = ar * ti + ai * tr
-    xscr[...] = jnp.dot(
+    xscr[0:128, :] = jnp.dot(
         lhs[...], outer_ref[...], precision=HIGHEST, preferred_element_type=jnp.float32
     )
     group = lax.broadcasted_iota(jnp.int32, (8, 128), 1) // 32
@@ -313,15 +314,21 @@
         return 0
 
     lax.fori_loop(0, 8, first, 0)
+    def second(cc):
+        for zz in range(8):
+            for s in range(4):
+                at = pl.multiple_of(128 * cc + 16 * zz, 16)
+                rows[s, pl.ds(at, 16), :] = bbuf[cc, zz, s].astype(jnp.float32)
+        for s in range(4):
+            for r in range(8):
+                for k in range(2):
+                    bf[r, s, k, pl.ds(pl.multiple_of(8 * cc, 8), 8), :] = rows[
+                        s, pl.ds(128 * cc + r + 8 * k, 8, stride=16), :
+                    ]
+
+    second(c)
     remote(bbuf.at[1 - c], bbuf.at[1 - c], s_d.at[2], r_d.at[2], sibling).wait_recv()
-
-    for b in range(16):
-        for s in range(4):
-            rows[s, 16 * b : 16 * b + 16, :] = bbuf[b // 8, b % 8, s].astype(jnp.float32)
-    for s in range(4):
-        for r in range(8):
-            bf[r, s, 0] = rows[s, pl.ds(r, 16, stride=16), :]
-            bf[r, s, 1] = rows[s, pl.ds(r + 8, 16, stride=16), :]
+    second(1 - c)
 
     mine = slot_of(me)
     for lo, hi in PARTS:
@@ -388,7 +395,7 @@
                 v = rbuf[s, at + 8 * cc : at + 8 * cc + 8, :]
                 turn_buf[n, pl.ds(to, 8, stride=8), :] = v.astype(jnp.float32)
         return lax.dot_general(
-            order, turn_buf[n].astype(jnp.bfloat16), (((1,), (1,)), ((), ())),
+            order, turn_buf[n, 0:128, :].astype(jnp.bfloat16), (((1,), (1,)), ((), ())),
             preferred_element_type=jnp.float32,
         )
 
@@ -434,7 +441,7 @@
             pltpu.VMEM(inverse.shape, bf16),
             pltpu.VMEM((10, 8, 128), f32),
             pltpu.VMEM((128, 256), f32),
-            pltpu.VMEM((128, 128), f32),
+            pltpu.VMEM((136, 128), f32),
             pltpu.VMEM((128, 128), f32),
             pltpu.VMEM((2, 40, 128), f32),
             pltpu.VMEM((2, 40, 128), f32),
@@ -446,7 +453,7 @@
             pltpu.VMEM((2, 8, 1, 128), f32),
             pltpu.VMEM((16, 4, 16, 128), bf16),
             pltpu.VMEM((2, 8, 4, 16, 128), bf16),
-            pltpu.VMEM((4, 256, 128), f32),
+            pltpu.VMEM((4, 272, 128), f32),
             pltpu.VMEM((16, 4, 16, 128), f32),
             pltpu.VMEM((8, 4, 2, 16, 128), f32),
             pltpu.VMEM((16, 128), f32),
@@ -454,7 +461,7 @@
             pltpu.VMEM((2, 256, BINS), bf16),
             pltpu.VMEM((8, ROWS, 128), bf16),
             pltpu.VMEM((8, ROWS, 128), bf16),
-            pltpu.VMEM((13, 128, 128), f32),
+            pltpu.VMEM((13, 136, 128), f32),
             dma((7,)), dma, dma((2,)), dma((2,)), dma((8,)), dma((8,)), dma((8,)), dma((8,)),
             dma((3,)), dma((3,)), dma((8,)), dma((8,)), dma((16,)), dma((16,)), dma((8,)), dma((8,)),
             dma((16,)), dma((16,)), dma((8,)), dma((8,)), dma((2, 8)), dma((2, 8)),

time: 37.8 us -> 37.5 us (level)
  no operation moved by 1% of the time
where the time goes in v7:
time: 37.5 us; the launch traced here: 37.4 us
  Pallas kernels  36.5 us (97%)
  local copies, waits for them, and re-layouts  0.89 us (2%)
    pallas_call x1, Pallas kernels, on_device(): pl.pallas_call(kernel, out_shape=jax.ShapeDtypeStruct((LAGS, 2, 128), f32...  36.5 us
    unnamed x1, local copies, waits for them, and re-layouts  0.89 us

profile of v7, /device:TPU:1, one launch (start us, length us, event | category | flops | bytes accessed | tf_op | source)
XLA Modules:
  0.0 37.4 jit_solution(18412233437826271394)
XLA Ops:
  0.0 36.5 %shard_map.82 = f32[801,2,128]{2,1,0:T(2,128)S(1)} custom-call(s32[2]{0:T(128)} %net_hbm.1, s32[2,2]{1,0:T(2,128)} %qual_hbm.1, f32[2,2400]{1,0:T(2,128)} %tr_hbm.1, f32[8,128]{1,0:T(8,128)} %bitcast.4, f32[8,128]{1,0:T(8,128)} %bitcast.5, f32[2,16,128]{2,1,0:T(8,128)} %constant.6.clone.tw_hbm, f32[256,128]{1,0:T(8,128)} %constant.7.clone.outer_hbm, ...), custom_call_target="tpu_custom_call" | custom-call | tf_op jit(solution)/shard_map/pallas_call | solution.py:430
  36.5 0.9 %copy.10 = f32[2,128,801]{1,0,2:T(2,128)} copy(f32[2,128,801]{1,0,2:T(2,128)S(1)} %bitcast.3) | data formatting | bytes 1640448

commit v8 on v7

--- a/solution.py
+++ b/solution.py
@@ -15,7 +15,7 @@
 LAGS = 2 * MAXLAG + 1
 ROWS = 208
 CHUNKS = ((0, 0, 128), (256, 128, 80))
-PARTS = ((0, 2), (2, 4), (4, 6), (6, 8))
+PARTS = ((0, 1), (1, 3), (3, 5), (5, 8))
 HIGHEST = lax.Precision.HIGHEST
 
 

time: 37.5 us -> 37.6 us (level)
  no operation moved by 1% of the time
where the time goes in v8:
time: 37.6 us; the launch traced here: 37.5 us
  Pallas kernels  36.6 us (97%)
  local copies, waits for them, and re-layouts  0.89 us (2%)
    pallas_call x1, Pallas kernels, on_device(): pl.pallas_call(kernel, out_shape=jax.ShapeDtypeStruct((LAGS, 2, 128), f32...  36.6 us
    unnamed x1, local copies, waits for them, and re-layouts  0.89 us

profile of v8, /device:TPU:1, one launch (start us, length us, event | category | flops | bytes accessed | tf_op | source)
XLA Modules:
  0.0 37.5 jit_solution(14516939019518994708)
XLA Ops:
  0.0 36.6 %shard_map.82 = f32[801,2,128]{2,1,0:T(2,128)S(1)} custom-call(s32[2]{0:T(128)} %net_hbm.1, s32[2,2]{1,0:T(2,128)} %qual_hbm.1, f32[2,2400]{1,0:T(2,128)} %tr_hbm.1, f32[8,128]{1,0:T(8,128)} %bitcast.4, f32[8,128]{1,0:T(8,128)} %bitcast.5, f32[2,16,128]{2,1,0:T(8,128)} %constant.6.clone.tw_hbm, f32[256,128]{1,0:T(8,128)} %constant.7.clone.outer_hbm, ...), custom_call_target="tpu_custom_call" | custom-call | tf_op jit(solution)/shard_map/pallas_call | solution.py:430
  36.6 0.9 %copy.10 = f32[2,128,801]{1,0,2:T(2,128)} copy(f32[2,128,801]{1,0,2:T(2,128)S(1)} %bitcast.3) | data formatting | bytes 1640448
